TPU v7x, 256 devices: a whole 4x4x8 slice. The times are simulated.
256 devices in a mesh: gx: 16 (over y, x), gy: 16 (over z, core).
Axes of the slice: x: 4, y: 4, z: 8, core: 2. Of those that a mesh axis runs over, the one named last changes fastest.
Arguments:
- coarse_state: float32 [7, 96, 96, 384], P(None, 'gx', 'gy')
- fine_state: float32 [7, 524288], P(None, ('gx', 'gy'))
- patch_source: int32 [16, 16, 4], replicated, may hold values from 0 to 15, as said below
- patch_live: int32 [16, 16, 4], replicated, may hold values from 0 to 1, as said below
Outputs:
- coarse_out: float32 [7, 96, 96, 384], P(None, 'gx', 'gy')
- fine_out: float32 [7, 524288], P(None, ('gx', 'gy'))
Inputs may be any that keep to these rules, and one draw needn't show every extreme that they name: For each gx index a and slot k, patch_source[a, :, k] names every gy index once; the live slots of one device name distinct tiles. A patch in slot k covers position k along the third dimension of its tile. `patch_live`: A device's live slots are its first ones; in every gx index at least one device has all 4 slots live, and every device has at least 1.
All inputs are finite; a program needn't handle non-finite values.
Results may differ from a plain program's by a relative error of at most 0.0003.
Values sent between devices are 32-bit elements; how exact they have to be, the bound alone decides.
A program may use at most 128 MiB of HBM per device.

v0:
```python
import jax
import jax.numpy as jnp
from jax import lax
from jax.sharding import PartitionSpec as P

FIELDS = 7
BOX = 4
CAP = 4


GAMMA_MINUS = 0.4
WAVE_SPEED = 4.0
COURANT = 0.05
BURN_RATE = 10.0
HEAT_RELEASE = 2.0


def padded_2(array, sides, width):
    for axis, dim in sides:
        size, length = (lax.axis_size(axis), array.shape[dim])
        up = [(i, (i + 1) % size) for i in range(size)]
        down = [(j, i) for i, j in up]
        last = lax.slice_in_dim(array, length - width, length, axis=dim)
        leading = lax.slice_in_dim(array, 0, width, axis=dim)
        before = lax.ppermute(last, axis, up)
        after = lax.ppermute(leading, axis, down)
        array = jnp.concatenate([before, array, after], axis=dim)
    return array


def minmod(first_arg, second_arg):
    return (
        0.5
        * (jnp.sign(first_arg) + jnp.sign(second_arg))
        * jnp.minimum(jnp.abs(first_arg), jnp.abs(second_arg))
    )


def euler_flux(fields, dim_index):
    density = fields[0]
    momentum = fields[1:4]
    velocity = fields[1 + dim_index] / density
    kinetic = (
        0.5
        * (momentum[0] * momentum[0] + momentum[1] * momentum[1] + momentum[2] * momentum[2])
        / density
    )
    pressure = GAMMA_MINUS * (fields[4] - kinetic)
    rows_out = [fields[1 + dim_index]]
    for spatial in range(3):
        flux_term = momentum[spatial] * velocity
        if spatial == dim_index:
            flux_term = flux_term + pressure
        rows_out.append(flux_term)
    rows_out.append((fields[4] + pressure) * velocity)
    rows_out.append(fields[5] * velocity)
    rows_out.append(fields[6] * velocity)
    return jnp.stack(rows_out)


def face_fluxes(fields, direction):
    length = fields.shape[direction]
    jumps = lax.slice_in_dim(fields, 1, length, axis=direction) - lax.slice_in_dim(
        fields, 0, length - 1, axis=direction
    )
    slopes = minmod(
        lax.slice_in_dim(jumps, 0, length - 2, axis=direction),
        lax.slice_in_dim(jumps, 1, length - 1, axis=direction),
    )
    left_state = lax.slice_in_dim(fields, 1, length - 2, axis=direction) + 0.5 * lax.slice_in_dim(
        slopes, 0, length - 3, axis=direction
    )
    right_state = lax.slice_in_dim(fields, 2, length - 1, axis=direction) - 0.5 * lax.slice_in_dim(
        slopes, 1, length - 2, axis=direction
    )
    return 0.5 * (
        euler_flux(left_state, direction - 1) + euler_flux(right_state, direction - 1)
    ) - 0.5 * WAVE_SPEED * (right_state - left_state)


def reaction(fields):
    burned = BURN_RATE * fields[5]
    nothing = jnp.zeros_like(burned)
    return jnp.stack([nothing, nothing, nothing, nothing, HEAT_RELEASE * burned, -burned, burned])


def advance(padded, tstep):
    interior = padded[:, 2:-2, 2:-2, 2:-2]
    flux_x = face_fluxes(padded[:, :, 2:-2, 2:-2], 1)
    flux_y = face_fluxes(padded[:, 2:-2, :, 2:-2], 2)
    flux_z = face_fluxes(padded[:, 2:-2, 2:-2, :], 3)
    change = (
        flux_x[:, 1:]
        - flux_x[:, :-1]
        + (flux_y[:, :, 1:] - flux_y[:, :, :-1])
        + (flux_z[:, :, :, 1:] - flux_z[:, :, :, :-1])
    )
    return (interior - COURANT * change + tstep * reaction(interior), flux_x, flux_y, flux_z)


def pair_across(face_values):
    slots = face_values.shape[2]
    return jnp.transpose(
        face_values.reshape(FIELDS, BOX, 2, slots, BOX, 2).sum(axis=(2, 5)), (0, 2, 1, 3)
    )


def pair_normal(face_values):
    slots = face_values.shape[3]
    return jnp.transpose(
        face_values.reshape(FIELDS, BOX, 2, BOX, 2, slots).sum(axis=(2, 4)), (0, 3, 1, 2)
    )


def fine_substep(work):
    padded_side = work.shape[1]
    slots = work.shape[3] // padded_side
    shape_five = (FIELDS, padded_side, padded_side, slots, padded_side)
    along_x = face_fluxes(work, 1).reshape(
        FIELDS, padded_side - 3, padded_side, slots, padded_side
    )[:, :, 2:-2, :, 2:-2]
    along_y = face_fluxes(work, 2).reshape(
        FIELDS, padded_side, padded_side - 3, slots, padded_side
    )[:, 2:-2, :, :, 2:-2]
    flat_z = face_fluxes(work, 3)
    before = jnp.zeros(flat_z.shape[:3] + (1,), flat_z.dtype)
    after = jnp.zeros(flat_z.shape[:3] + (2,), flat_z.dtype)
    along_z = jnp.concatenate([before, flat_z, after], axis=3).reshape(shape_five)[
        :, 2:-2, 2:-2, :, 1 : padded_side - 2
    ]
    interior = work.reshape(shape_five)[:, 2:-2, 2:-2, :, 2:-2]
    change = (
        along_x[:, 1:]
        - along_x[:, :-1]
        + (along_y[:, :, 1:] - along_y[:, :, :-1])
        + (along_z[..., 1:] - along_z[..., :-1])
    )
    updated = interior - COURANT * change + 0.5 * COURANT * reaction(interior)
    faces = jnp.stack(
        [
            pair_across(along_x[:, 0]),
            pair_across(along_x[:, -1]),
            pair_across(along_y[:, :, 0]),
            pair_across(along_y[:, :, -1]),
            pair_normal(along_z[..., 0]),
            pair_normal(along_z[..., -1]),
        ],
        axis=1,
    )
    return (updated, faces)


def fill_block(ghost, interior):
    slots = ghost.shape[0]
    spread = jnp.transpose(ghost, (1, 2, 3, 0, 4))
    spread = jnp.repeat(jnp.repeat(jnp.repeat(spread, 2, axis=1), 2, axis=2), 2, axis=4)
    spread = spread.at[:, 2:-2, 2:-2, :, 2:-2].set(interior)
    return spread.reshape(FIELDS, spread.shape[1], spread.shape[2], slots * spread.shape[4])


def correct(work, position, coarse_face, fine_face, live, lower_face):
    cell_value = work[position]
    if lower_face:
        moved = cell_value + COURANT * (coarse_face - fine_face)
    else:
        moved = cell_value + COURANT * (fine_face - coarse_face)
    return work.at[position].set(jnp.where(live, moved, cell_value))


def local(coarse_state, fine_state, patch_source, patch_live):
    coarse_side = BOX + 2
    fine_side = 2 * BOX
    zslots = coarse_state.shape[3] // coarse_side
    highest = lax.Precision.HIGHEST
    my_row = lax.axis_index("gx")
    my_col = lax.axis_index("gy")
    groups = lax.axis_size("gy")
    owners = jnp.arange(groups, dtype=jnp.int32)
    row_source = jnp.take(patch_source, my_row, axis=0)
    row_live = jnp.take(patch_live, my_row, axis=0)
    sending = ((row_source == my_col) & (row_live == 1)).astype(jnp.float32)
    own_source = jnp.take(row_source, my_col, axis=0)
    own_live = jnp.take(row_live, my_col, axis=0) == 1
    rimmed = padded_2(coarse_state, (("gx", 1), ("gy", 2)), 2)
    rimmed = jnp.concatenate([rimmed[..., -2:], rimmed, rimmed[..., :2]], axis=3)
    advanced, flux_x, flux_y, flux_z = advance(rimmed, COURANT)

    def slot_blocks(tile):
        return jnp.transpose(
            tile.reshape(FIELDS, coarse_side, coarse_side, zslots, coarse_side)[:, :, :, :CAP],
            (3, 0, 1, 2, 4),
        )

    old_blocks = slot_blocks(coarse_state)
    new_blocks = slot_blocks(advanced)
    sent_old = jnp.einsum("jk,kfxyz->jfxyz", sending, old_blocks, precision=highest)
    sent_new = jnp.einsum("jk,kfxyz->jfxyz", sending, new_blocks, precision=highest)
    got_old, got_new = (
        lax.all_to_all(sent_old, "gy", split_axis=0, concat_axis=0, tiled=True),
        lax.all_to_all(sent_new, "gy", split_axis=0, concat_axis=0, tiled=True),
    )
    ghost_old = jnp.take(got_old, own_source, axis=0)
    ghost_new = jnp.take(got_new, own_source, axis=0)
    live_ghost = own_live[:, None, None, None, None]
    ghost_old = jnp.where(live_ghost, ghost_old, 1.0)
    ghost_new = jnp.where(live_ghost, ghost_new, 1.0)
    fine_now = jnp.transpose(
        fine_state.reshape(FIELDS, CAP, fine_side, fine_side, fine_side), (0, 2, 3, 1, 4)
    )
    first, faces_one = fine_substep(fill_block(ghost_old, fine_now))
    second, faces_two = fine_substep(fill_block(0.5 * (ghost_old + ghost_new), first))
    fine_kept = jnp.where(own_live[None, None, None, :, None], second, fine_now)
    fine_out = jnp.transpose(fine_kept, (0, 3, 1, 2, 4)).reshape(
        FIELDS, CAP * fine_side * fine_side * fine_side
    )
    averaged = second.reshape(FIELDS, BOX, 2, BOX, 2, CAP, BOX, 2).mean(axis=(2, 4, 7))
    registers = 0.125 * (faces_one + faces_two)
    returning = ((own_source[None, :] == owners[:, None]) & own_live[None, :]).astype(jnp.float32)
    out_avg = jnp.einsum("jk,fxykz->jfxyz", returning, averaged, precision=highest)
    out_reg = jnp.einsum("jk,fakbc->jfabc", returning, registers, precision=highest)
    got_avg, got_reg = (
        lax.all_to_all(out_avg, "gy", split_axis=0, concat_axis=0, tiled=True),
        lax.all_to_all(out_reg, "gy", split_axis=0, concat_axis=0, tiled=True),
    )
    slot_avg = jnp.einsum("jk,jfxyz->fxykz", sending, got_avg, precision=highest)
    slot_reg = jnp.einsum("jk,jfabc->fakbc", sending, got_reg, precision=highest)
    slot_live = jnp.sum(sending, axis=0) > 0.5
    slab = advanced.reshape(FIELDS, coarse_side, coarse_side, zslots, coarse_side)
    work = slab[:, :, :, :CAP]
    flux_x5 = flux_x.reshape(FIELDS, coarse_side + 1, coarse_side, zslots, coarse_side)[
        :, :, :, :CAP
    ]
    flux_y5 = flux_y.reshape(FIELDS, coarse_side, coarse_side + 1, zslots, coarse_side)[
        :, :, :, :CAP
    ]
    flux_z5 = flux_z[..., : zslots * coarse_side].reshape(
        FIELDS, coarse_side, coarse_side, zslots, coarse_side
    )[:, :, :, :CAP]
    inside = slice(1, BOX + 1)
    far_end = BOX + 1
    whole = slice(None)
    interior = work[:, inside, inside, :, inside]
    work = work.at[:, inside, inside, :, inside].set(
        jnp.where(slot_live[None, None, None, :, None], slot_avg, interior)
    )
    live_across = slot_live[None, None, :, None]
    live_normal = slot_live[None, None, None, :]
    across_x = [jnp.transpose(slot_reg[:, index_face], (0, 2, 1, 3)) for index_face in range(4)]
    normal_z = [jnp.transpose(slot_reg[:, index_face], (0, 2, 3, 1)) for index_face in range(4, 6)]
    work = correct(
        work,
        (whole, 0, inside, whole, inside),
        flux_x5[:, 1, inside, :, inside],
        across_x[0],
        live_across,
        True,
    )
    work = correct(
        work,
        (whole, far_end, inside, whole, inside),
        flux_x5[:, far_end, inside, :, inside],
        across_x[1],
        live_across,
        False,
    )
    work = correct(
        work,
        (whole, inside, 0, whole, inside),
        flux_y5[:, inside, 1, :, inside],
        across_x[2],
        live_across,
        True,
    )
    work = correct(
        work,
        (whole, inside, far_end, whole, inside),
        flux_y5[:, inside, far_end, :, inside],
        across_x[3],
        live_across,
        False,
    )
    work = correct(
        work,
        (whole, inside, inside, whole, 0),
        flux_z5[:, inside, inside, :, 1],
        normal_z[0],
        live_normal,
        True,
    )
    work = correct(
        work,
        (whole, inside, inside, whole, far_end),
        flux_z5[:, inside, inside, :, far_end],
        normal_z[1],
        live_normal,
        False,
    )
    slab = slab.at[:, :, :, :CAP].set(work)
    coarse_out = slab.reshape(advanced.shape)
    return (coarse_out, fine_out)


def solution(mesh):
    return jax.shard_map(
        local,
        mesh=mesh,
        in_specs=(P(None, "gx", "gy", None), P(None, ("gx", "gy")), P(), P()),
        out_specs=(P(None, "gx", "gy", None), P(None, ("gx", "gy"))),
        check_vma=False,
    )
```

profile of v0, /device:TPU:1, one launch (start us, length us, event | category | flops | bytes accessed | tf_op | source)
XLA Modules:
  0.0 495.8 jit_solution(8466825193762256417)
XLA Ops:
  4.0 3.8 collective-permute-start.1
  7.8 10.8 %reshape.549 = f32[7,6,6,64,6]{4,3,0,2,1:T(8,128)} reshape(f32[7,6,6,384]{3,0,2,1:T(8,128)} %param.30) | data formatting | bytes 774144 | tf_op jit(solution)/shard_map/reshape | solution.py:190
  25.2 3.7 reshape.697
  28.9 9.7 %all-to-all-start = ((f32[16,1,1512]{2,1,0:T(1,128)}), f32[16,1,1512]{2,1,0:T(1,128)S(1)}, u32[]{:S(2)}, u32[]{:S(2)}) async-start(f32[16,1,1512]{2,1,0:T(1,128)} %reshape.697), calls=%async_computation | async-start | bytes 196608 | tf_op jit(solution)/shard_map/all_to_all | solution.py:199
  47.8 11.8 %reshape.565 = f32[7,7,6,64,6]{4,3,1,2,0:T(8,128)} reshape(f32[7,7,6,384]{3,1,2,0:T(8,128)S(1)} %multiply_subtract_fusion.4) | data formatting | bytes 903168 | tf_op jit(solution)/shard_map/reshape | solution.py:230
  66.2 5.9 %copy.214 = f32[16,7,6,6,6]{4,1,3,2,0:T(8,128)} copy(f32[16,7,6,6,6]{1,4,3,2,0:T(8,128)} %bitcast.279) | data formatting | bytes 193536 | tf_op jit(solution)/shard_map/all_to_all | solution.py:199
  72.1 3.1 gather_fusion
  81.5 10.1 %reshape.547 = f32[7,6,6,64,6]{4,3,0,2,1:T(8,128)} reshape(f32[7,6,6,384]{3,0,2,1:T(8,128)S(1)} %copy.210) | data formatting | bytes 774144 | tf_op jit(solution)/shard_map/reshape | solution.py:228
  94.2 14.0 %reshape.692 = f32[7,6,7,64,6]{4,3,1,2,0:T(8,128)} reshape(f32[7,6,7,384]{3,1,2,0:T(8,128)S(1)} %multiply_subtract_fusion.1) | data formatting | bytes 903168 | tf_op jit(solution)/shard_map/reshape | solution.py:233
  108.2 10.2 %reshape.693 = f32[7,6,6,64,6]{4,3,1,2,0:T(8,128)} reshape(f32[7,6,6,384]{3,1,2,0:T(8,128)S(1)} %get-tuple-element.281) | data formatting | bytes 774144 | tf_op jit(solution)/shard_map/reshape | solution.py:236
  126.8 2.9 copy.226
  131.8 8.5 %all-to-all-start.1 = ((f32[16,1,1512]{2,1,0:T(1,128)}), f32[16,1,1512]{2,1,0:T(1,128)S(1)}, u32[]{:S(2)}, u32[]{:S(2)}) async-start(f32[16,1,1512]{2,1,0:T(1,128)} %reshape.699), calls=%async_computation.1 | async-start | bytes 196608 | tf_op jit(solution)/shard_map/all_to_all | solution.py:200
  143.0 5.8 %all-to-all-done.1 = f32[16,1,1512]{2,1,0:T(1,128)S(1)} async-done(((f32[16,1,1512]{2,1,0:T(1,128)}), f32[16,1,1512]{2,1,0:T(1,128)S(1)}, u32[]{:S(2)}, u32[]{:S(2)}) %all-to-all-start.1) | async-done | bytes 96800 | tf_op jit(solution)/shard_map/all_to_all | solution.py:200
  152.2 4.8 copy.227
  167.6 74.3 %scatter.34 = f32[7,12,12,4,12]{2,3,4,1,0:T(4,128)S(1)} dynamic-update-slice(f32[7,12,12,4,12]{2,3,4,1,0:T(4,128)S(1)} %bitcast.283, f32[7,8,8,4,8]{2,3,4,1,0:T(4,128)} %copy.218, s32[]{:T(128)} %constant.415.clone.1, s32[]{:T(128)} %constant.416.clone.1, s32[]{:T(128)} %constant.416.clone.1, s32[]{:T(128)} %constant.415.clone.1, s32[]{:T(128)} %constant.416.clone.1) | dynamic-update-slice | bytes 114692 | tf_op jit(solution)/shard_map/scatter | solution.py:157
  241.9 3.4 copy.219
  300.1 74.3 %scatter.35 = f32[7,12,12,4,12]{2,3,4,1,0:T(4,128)S(1)} dynamic-update-slice(f32[7,12,12,4,12]{2,3,4,1,0:T(4,128)S(1)} %bitcast.282, f32[7,8,8,4,8]{2,3,4,1,0:T(4,128)} %copy.231, s32[]{:T(128)} %constant.415.clone.1, s32[]{:T(128)} %constant.416.clone.1, s32[]{:T(128)} %constant.416.clone.1, s32[]{:T(128)} %constant.415.clone.1, s32[]{:T(128)} %constant.416.clone.1) | dynamic-update-slice | bytes 114692 | tf_op jit(solution)/shard_map/scatter | solution.py:157
  374.4 3.4 copy.232
  449.5 4.3 select_bitcast_fusion
  459.9 3.6 all-to-all-start.2
  468.0 2.8 all-to-all-done.2
  470.8 4.4 all-to-all-start.3
  477.2 5.5 %all-to-all-done.3 = f32[16,1,672]{2,1,0:T(1,128)S(1)} async-done(((f32[16,1,672]{2,1,0:T(1,128)}), f32[16,1,672]{2,1,0:T(1,128)S(1)}, u32[]{:S(2)}, u32[]{:S(2)}) %all-to-all-start.3) | async-done | bytes 43040 | tf_op jit(solution)/shard_map/all_to_all | solution.py:223
  487.8 7.7 %reshape.574 = f32[7,6,6,384]{3,0,2,1:T(8,128)} reshape(f32[7,6,6,64,6]{4,3,0,2,1:T(8,128)} %constant_dynamic-update-slice_fusion.54) | data formatting | bytes 774144 | tf_op jit(solution)/shard_map/reshape | solution.py:299
  (379 shorter events, 204.4 us)
Async XLA Ops:
  1.9 41.8 %collective-permute-start = (f32[7,2,6,384]{3,1,2,0:T(2,128)S(1)}, f32[7,2,6,384]{3,1,2,0:T(2,128)S(1)}, u32[]{:S(2)}, u32[]{:S(2)}) collective-permute-start(f32[7,2,6,384]{3,1,2,0:T(2,128)S(1)} %get-tuple-element.308), channel_id=1, source_target_pairs={{0,16},{16,32},{32,48},{48,64},{64,80},{80,96},{96,112},{112,128},... | collective-permute-start | bytes 387080 | tf_op jit(solution)/shard_map/ppermute | solution.py:25
  4.0 39.7 %collective-permute-start.1 = (f32[7,2,6,384]{3,1,2,0:T(2,128)S(1)}, f32[7,2,6,384]{3,1,2,0:T(2,128)S(1)}, u32[]{:S(2)}, u32[]{:S(2)}) collective-permute-start(f32[7,2,6,384]{3,1,2,0:T(2,128)S(1)} %get-tuple-element.309), channel_id=1, source_target_pairs={{16,0},{32,16},{48,32},{64,48},{80,64},{96,80},{112,96},{128,112},... | collective-permute-start | bytes 387080 | tf_op jit(solution)/shard_map/ppermute | solution.py:26
  25.2 14.9 %copy-start.41 = (f32[7,2048]{1,0:T(8,128)S(1)}, f32[7,2048]{1,0:T(8,128)}, u32[]{:S(2)}) copy-start(f32[7,2048]{1,0:T(8,128)} %param.31) | copy-start | bytes 172036
  28.9 33.4 %all-to-all-start = ((f32[16,1,1512]{2,1,0:T(1,128)}), f32[16,1,1512]{2,1,0:T(1,128)S(1)}, u32[]{:S(2)}, u32[]{:S(2)}) async-start(f32[16,1,1512]{2,1,0:T(1,128)} %reshape.697), calls=%async_computation | async-start | bytes 196608 | tf_op jit(solution)/shard_map/all_to_all | solution.py:199
  43.7 36.6 %copy-start.42 = (f32[7]{0:T(128)}, f32[7]{0:T(128)S(1)}, u32[]{:S(2)}) copy-start(f32[7]{0:T(128)S(1)} %pad.56.clone) | copy-start | bytes 88
  45.3 29.9 %collective-permute-start.2 = (f32[7,10,2,384]{3,1,2,0:T(8,128)}, f32[7,10,2,384]{3,1,2,0:T(8,128)S(1)}, u32[]{:S(2)}, u32[]{:S(2)}) collective-permute-start(f32[7,10,2,384]{3,1,2,0:T(8,128)} %get-tuple-element.273), channel_id=1, source_target_pairs={{0,1},{1,2},{2,3},{3,4},{4,5},{5,6},{6,7},{7,8},{8,9},{9,10},{10,1... | collective-permute-start | bytes 645128 | tf_op jit(solution)/shard_map/ppermute | solution.py:25
  47.0 28.2 %collective-permute-start.3 = (f32[7,10,2,384]{3,1,2,0:T(8,128)}, f32[7,10,2,384]{3,1,2,0:T(8,128)S(1)}, u32[]{:S(2)}, u32[]{:S(2)}) collective-permute-start(f32[7,10,2,384]{3,1,2,0:T(8,128)} %get-tuple-element.274), channel_id=1, source_target_pairs={{1,0},{2,1},{3,2},{4,3},{5,4},{6,5},{7,6},{8,7},{9,8},{10,9},{11,1... | collective-permute-start | bytes 645128 | tf_op jit(solution)/shard_map/ppermute | solution.py:26
  131.8 17.0 %all-to-all-start.1 = ((f32[16,1,1512]{2,1,0:T(1,128)}), f32[16,1,1512]{2,1,0:T(1,128)S(1)}, u32[]{:S(2)}, u32[]{:S(2)}) async-start(f32[16,1,1512]{2,1,0:T(1,128)} %reshape.699), calls=%async_computation.1 | async-start | bytes 196608 | tf_op jit(solution)/shard_map/all_to_all | solution.py:200
  424.6 8.1 %copy-start.11 = (f32[7,8,8,4,1]{4,3,0,2,1:T(4,128)S(1)}, f32[7,8,8,4,1]{4,3,0,2,1:T(4,128)}, u32[]{:S(2)}) copy-start(f32[7,8,8,4,1]{4,3,0,2,1:T(4,128)} %get-tuple-element.234) | copy-start | bytes 21508
  425.0 12.0 %copy-start.22 = (f32[7,1,8,4,8]{4,3,0,2,1:T(4,128)S(1)}, f32[7,1,8,4,8]{4,3,0,2,1:T(4,128)}, u32[]{:S(2)}) copy-start(f32[7,1,8,4,8]{4,3,0,2,1:T(4,128)} %get-tuple-element.244) | copy-start | bytes 21508
  435.0 14.5 %copy-start.1 = (f32[7,8,8,4,8]{4,2,1,3,0:T(8,128)S(1)}, f32[7,8,8,4,8]{4,2,1,3,0:T(8,128)}, u32[]{:S(2)}) copy-start(f32[7,8,8,4,8]{4,2,1,3,0:T(8,128)} %copy-done) | copy-start | bytes 172036
  435.0 14.5 %copy-start.9 = (f32[7,8,8,4,8]{4,3,0,2,1:T(4,128)S(1)}, f32[7,8,8,4,8]{4,3,0,2,1:T(4,128)}, u32[]{:S(2)}) copy-start(f32[7,8,8,4,8]{4,3,0,2,1:T(4,128)} %get-tuple-element.249) | copy-start | bytes 172036
  435.0 14.5 %copy-start.18 = (f32[1,8,8,4,8]{4,2,1,3,0:T(8,128)S(1)}, f32[1,8,8,4,8]{4,2,1,3,0:T(8,128)}, u32[]{:S(2)}) copy-start(f32[1,8,8,4,8]{4,2,1,3,0:T(8,128)} %get-tuple-element.277) | copy-start | bytes 24580
  456.6 7.2 %copy-start.32 = (f32[7,4,4,4]{0,2,3,1:T(4,128)S(1)}, f32[7,4,4,4]{0,2,3,1:T(4,128)}, u32[]{:S(2)}) copy-start(f32[7,4,4,4]{0,2,3,1:T(4,128)} %reduce_sum.139) | copy-start | bytes 5380
  459.9 10.9 %all-to-all-start.2 = ((f32[16,1,448]{2,1,0:T(1,128)}), f32[16,1,448]{2,1,0:T(1,128)S(1)}, u32[]{:S(2)}, u32[]{:S(2)}) async-start(f32[16,1,448]{2,1,0:T(1,128)} %reshape.701), calls=%async_computation.2 | async-start | bytes 65536 | tf_op jit(solution)/shard_map/all_to_all | solution.py:222
  463.9 12.7 %copy-start.5 = (f32[7,6,6,4,6]{0,3,4,2,1:T(4,128)S(1)}, f32[7,6,6,4,6]{0,3,4,2,1:T(4,128)}, u32[]{:S(2)}) copy-start(f32[7,6,6,4,6]{0,3,4,2,1:T(4,128)} %copy-done.4) | copy-start | bytes 72580
  463.9 12.7 %copy-start.19 = (f32[7,4,4,4,4]{0,3,4,2,1:T(4,128)S(1)}, f32[7,4,4,4,4]{0,3,4,2,1:T(4,128)}, u32[]{:S(2)}) copy-start(f32[7,4,4,4,4]{0,3,4,2,1:T(4,128)} %copy.299) | copy-start | bytes 21508
  466.4 18.7 %copy-start.36 = (f32[7,1,4,4,4]{0,3,4,2,1:T(4,128)S(1)}, f32[7,1,4,4,4]{0,3,4,2,1:T(4,128)}, u32[]{:S(2)}) copy-start(f32[7,1,4,4,4]{0,3,4,2,1:T(4,128)} %copy.300) | copy-start | bytes 5380
  466.4 18.8 %copy-start.35 = (f32[7,1,4,4,4]{0,3,4,2,1:T(4,128)S(1)}, f32[7,1,4,4,4]{0,3,4,2,1:T(4,128)}, u32[]{:S(2)}) copy-start(f32[7,1,4,4,4]{0,3,4,2,1:T(4,128)} %copy.301) | copy-start | bytes 5380
  468.0 17.4 %copy-start.38 = (f32[7,4,1,4,4]{0,3,4,1,2:T(4,128)S(1)}, f32[7,4,1,4,4]{0,3,4,1,2:T(4,128)}, u32[]{:S(2)}) copy-start(f32[7,4,1,4,4]{0,3,4,1,2:T(4,128)} %copy.303) | copy-start | bytes 5380
  468.0 17.5 %copy-start.37 = (f32[7,4,1,4,4]{0,3,4,1,2:T(4,128)S(1)}, f32[7,4,1,4,4]{0,3,4,1,2:T(4,128)}, u32[]{:S(2)}) copy-start(f32[7,4,1,4,4]{0,3,4,1,2:T(4,128)} %copy.305) | copy-start | bytes 5380
  470.8 11.9 %all-to-all-start.3 = ((f32[16,1,672]{2,1,0:T(1,128)}), f32[16,1,672]{2,1,0:T(1,128)S(1)}, u32[]{:S(2)}, u32[]{:S(2)}) async-start(f32[16,1,672]{2,1,0:T(1,128)} %reshape.703), calls=%async_computation.3 | async-start | bytes 98304 | tf_op jit(solution)/shard_map/all_to_all | solution.py:223
  475.9 9.7 %copy-start.40 = (f32[7,4,4,4,1]{0,3,2,1,4:T(4,128)S(1)}, f32[7,4,4,4,1]{0,3,2,1,4:T(4,128)}, u32[]{:S(2)}) copy-start(f32[7,4,4,4,1]{0,3,2,1,4:T(4,128)} %copy.307) | copy-start | bytes 5380
  475.9 9.8 %copy-start.39 = (f32[7,4,4,4,1]{0,3,2,1,4:T(4,128)S(1)}, f32[7,4,4,4,1]{0,3,2,1,4:T(4,128)}, u32[]{:S(2)}) copy-start(f32[7,4,4,4,1]{0,3,2,1,4:T(4,128)} %copy.309) | copy-start | bytes 5380
  (31 other events, 110.4 us)
where the time goes:
time: 503 us; the launch traced here: 496 us
  local copies, waits for them, and re-layouts  376 us (75%)
  other arithmetic  64.6 us (13%)
  starting transfers between devices  33.9 us (7%)
  waiting for transfers between devices  14.1 us (3%)
  matrix products  5.06 us (1%)
    scatter x4, local copies, waits for them, and re-layouts, fill_block(): spread = spread.at[:, 2:-2, 2:-2, :, 2:-2].set(interior)  155 us
    unnamed x128, local copies, waits for them, and re-layouts  28.4 us
    another operation x12, local copies, waits for them, and re-layouts, euler_flux(): return jnp.stack(rows_out)  19.1 us
    reshape x1, local copies, waits for them, and re-layouts, local(): flux_y.reshape(FIELDS, coarse_side, coarse_side + 1, zslots, coarse_side)  14 us
    reshape x1, local copies, waits for them, and re-layouts, local(): flux_x.reshape(FIELDS, coarse_side + 1, coarse_side, zslots, coarse_side)  11.8 us
    reshape x1, local copies, waits for them, and re-layouts, slot_blocks(): tile.reshape(FIELDS, coarse_side, coarse_side, zslots, coarse_side)  10.8 us
    reshape x1, local copies, waits for them, and re-layouts, local(): flux_z[..., :zslots * coarse_side]  10.2 us
    reshape x1, local copies, waits for them, and re-layouts, local(): advanced.reshape(FIELDS, coarse_side, coarse_side, zslots, coarse_side)  10.1 us
  transfers between devices with their start and end apart: 8, of which 3 were waited for; matrix products, arithmetic and copies ran while one was open for 13% of the time, Pallas kernels for 0%

commit v1 on v0

v1 whole, which is shorter than its diff:
```python
import jax
import jax.numpy as jnp
from jax import lax
from jax.experimental import pallas as pl
from jax.experimental.pallas import tpu as pltpu
from jax.sharding import PartitionSpec as P

F = 7
CAP = 4
SIDE = 6
L = 128
F32 = jnp.float32
BF16 = jnp.bfloat16
MESH = pl.DeviceIdType.MESH


def iota(shape, dim):
    return lax.broadcasted_iota(jnp.int32, shape, dim)


def take(ref, start, count, stride):
    return ref.reshape(ref.size // L, L)[pl.ds(start, count, stride=stride), :]


def put(ref, start, count, stride, value):
    ref.reshape(ref.size // L, L)[pl.ds(start, count, stride=stride), :] = value


def exact_dot(a, e):
    hi = a.astype(BF16)
    rest = a - hi.astype(F32)
    mid = rest.astype(BF16)
    low = (rest - mid.astype(F32)).astype(BF16)
    out = jnp.dot(hi, e, preferred_element_type=F32)
    out = out + jnp.dot(mid, e, preferred_element_type=F32)
    return out + jnp.dot(low, e, preferred_element_type=F32)


def minmod(a, b):
    return jnp.maximum(jnp.minimum(a, b), 0.0) + jnp.minimum(jnp.maximum(a, b), 0.0)


def half_flux(u, d):
    inv = 1.0 / u[0]
    kk = u[1] * u[1] + u[2] * u[2] + u[3] * u[3]
    p = 0.4 * u[4] - 0.2 * (kk * inv)
    scaled = 0.025 * u[1 + d]
    v = scaled * inv
    out = [scaled]
    for i in range(3):
        term = u[1 + i] * v
        if i == d:
            term = term + 0.025 * p
        out.append(term)
    out += [(u[4] + p) * v, u[5] * v, u[6] * v]
    return out


def split_flux(um, u, up, d):
    h = [0.5 * minmod(c - m, q - c) for m, c, q in zip(um, u, up)]
    left = [c + s for c, s in zip(u, h)]
    right = [c - s for c, s in zip(u, h)]
    plus = [f + 0.1 * c for f, c in zip(half_flux(left, d), left)]
    minus = [f - 0.1 * c for f, c in zip(half_flux(right, d), right)]
    return plus, minus


def react(u, change, t):
    burned = (10.0 * t) * u[5]
    new = [c - g for c, g in zip(u, change)]
    new[4] = new[4] + 2.0 * burned
    new[5] = new[5] - burned
    new[6] = new[6] + burned
    return new


def make_kernel(n_gx, n_gy):
    def kernel(
        coarse, fine, source, live, coarse_out, fine_out,
        S, FIN, BASE, NEWC, WN, PZ, MZ, CM, BB, MO, MN, GL, FS, FT, GG, SB1, RB1, SB2, RB2,
        EZ, EG, WD, WX, E2, E2X, LW, TT, src_s, live_s, kf_s, kg_s,
        in_sem, fin_sem, tab_sem, h_send, h_recv, m_send, m_recv,
    ):
        a = lax.axis_index("gx")
        b = lax.axis_index("gy")
        up_a, dn_a = lax.rem(a + 1, n_gx), lax.rem(a + n_gx - 1, n_gx)
        up_b, dn_b = lax.rem(b + 1, n_gy), lax.rem(b + n_gy - 1, n_gy)

        tabs = [
            pltpu.make_async_copy(source.at[a], src_s, tab_sem.at[0]),
            pltpu.make_async_copy(live.at[a], live_s, tab_sem.at[1]),
        ]
        for cp in tabs:
            cp.start()
        own = []
        for j in range(3):
            cp = pltpu.make_async_copy(
                coarse.at[:, :, :, pl.ds(j * L, L)],
                S.at[2:8, 2:8, j, 0:F, :],
                in_sem.at[j],
            )
            cp.start()
            own.append(cp)
        fin_cp = pltpu.make_async_copy(fine, FIN, fin_sem)
        fin_cp.start()

        barrier = pltpu.get_barrier_semaphore()
        for d in (up_a, dn_a):
            pl.semaphore_signal(barrier, inc=1, device_id=(d, b), device_id_type=MESH)

        def greet(o, _):
            pl.semaphore_signal(
                barrier, inc=1, device_id=(a, lax.rem(b + o, n_gy)), device_id_type=MESH
            )
            return 0

        lax.fori_loop(1, n_gy, greet, 0)

        row = iota((L, L), 0)
        col = iota((L, L), 1)
        c32 = col & 31
        s32 = col >> 5
        zc = jnp.where(
            c32 < 4, 0, jnp.where(c32 < 8, 5, jnp.where(c32 < 12, c32 - 7, jnp.where(c32 < 16, c32 - 11, (c32 & 3) + 1)))
        )
        EZ[...] = (row == 6 * s32 + zc).astype(F32).astype(BF16)
        fy = (col >> 3) & 7
        fz = col & 7
        cz, cy = fz >> 1, fy >> 1
        EG[:, 0:L] = (row == jnp.where(fz < 4, 0, 4) + cy).astype(F32).astype(BF16)
        EG[:, L : 2 * L] = (row == jnp.where(fy < 4, 8, 12) + cz).astype(F32).astype(BF16)
        EG[:, 2 * L : 3 * L] = (row == 16 + cy * 4 + cz).astype(F32).astype(BF16)
        ry = (row >> 3) & 7
        rz = row & 7
        rzc, ryc = rz >> 1, ry >> 1
        e6 = (c32 * 43) >> 8
        eyv = jnp.where(c32 < 24, e6 + 1, jnp.where(c32 < 28, 0, 5))
        ezv = jnp.where(c32 < 24, c32 - 6 * e6, (c32 & 3) + 1)
        main = c32 < 24
        wa = main & (ezv >= 1) & (ezv <= 4) & (ryc == eyv - 1) & (rzc == ezv - 1)
        wz = main & (ryc == eyv - 1) & (((ezv == 0) & (rz == 0)) | ((ezv == 5) & (rz == 7)))
        wy = (
            jnp.logical_not(main)
            & (rzc == ezv - 1)
            & (((eyv == 0) & (ry == 0)) | ((eyv == 5) & (ry == 7)))
        )
        for i, w in enumerate((wa, wz, wy)):
            WD[i * L : (i + 1) * L, :] = jnp.where(w, 0.125, 0.0).astype(BF16)
        WX[...] = jnp.where((ryc == (c32 >> 2)) & (rzc == (c32 & 3)), 0.125, 0.0).astype(BF16)
        r32 = row & 31
        rs = row >> 5
        r6 = (r32 * 43) >> 8
        rzv = jnp.where(r32 < 24, r32 - 6 * r6, (r32 & 3) + 1)
        E2[...] = (col == 6 * rs + rzv).astype(F32).astype(BF16)
        E2X[...] = (col == 6 * rs + (r32 & 3) + 1).astype(F32).astype(BF16)

        for cp in tabs:
            cp.wait()

        def route(o, carry):
            owner, alive = carry
            d = lax.rem(b + o, n_gy)
            kf = jnp.int32(0)
            kg = jnp.int32(0)
            back = lax.rem(n_gy - o, n_gy)
            own_new, live_new = [], []
            for k in reversed(range(CAP)):
                kf = jnp.where((src_s[k, b] == d) & (live_s[k, b] == 1), k, kf)
                mine = src_s[k, d] == b
                lv = live_s[k, d]
                kg = jnp.where(mine & (lv == 1), k, kg)
                own_new.append(jnp.where(mine, back, owner[k]))
                live_new.append(jnp.where(mine, lv, alive[k]))
            kf_s[o] = kf
            kg_s[o] = kg
            return tuple(reversed(own_new)), tuple(reversed(live_new))

        zeros = (jnp.int32(0),) * CAP
        owner, alive = lax.fori_loop(0, n_gy, route, (zeros, zeros))

        for cp in own:
            cp.wait()
        pl.semaphore_wait(barrier, n_gy + 1)

        halos = []
        for j in range(3):
            for h, (src_x, dst_x, src_y, dst_y, dev) in enumerate(
                (
                    ((6, 8), (0, 2), (2, 8), (2, 8), (up_a, b)),
                    ((2, 4), (8, 10), (2, 8), (2, 8), (dn_a, b)),
                    ((2, 8), (2, 8), (6, 8), (0, 2), (a, up_b)),
                    ((2, 8), (2, 8), (2, 4), (8, 10), (a, dn_b)),
                )
            ):
                cp = pltpu.make_async_remote_copy(
                    src_ref=S.at[src_x[0] : src_x[1], src_y[0] : src_y[1], j, 0:F, :],
                    dst_ref=S.at[dst_x[0] : dst_x[1], dst_y[0] : dst_y[1], j, 0:F, :],
                    send_sem=h_send.at[j, h],
                    recv_sem=h_recv.at[j, h],
                    device_id=dev,
                    device_id_type=MESH,
                )
                cp.start()
                halos.append(cp)

        lane = iota((8, L), 1)
        sub = iota((8, L), 0)
        lc = lane & 31
        ls = lane >> 5
        ly = jnp.where(
            lc < 4, lc + 1, jnp.where(lc < 8, lc - 3, jnp.where(lc < 12, 0, jnp.where(lc < 16, 5, ((lc - 16) >> 2) + 1)))
        )
        low16 = lc < 16

        def ghost_messages(tiles, dst):
            BB[...] = exact_dot(tiles.reshape(SIDE * SIDE * 8, L), EZ[...]).reshape(SIDE, SIDE, 8, L)
            merged = []
            for X in range(4):
                acc = BB[X + 1, 0]
                for y in range(1, 6):
                    acc = jnp.where(low16 & (ly == y), BB[X + 1, y], acc)
                if X in (0, 3):
                    for y in range(1, 5):
                        acc = jnp.where(
                            jnp.logical_not(low16) & (ly == y), BB[0 if X == 0 else 5, y], acc
                        )
                merged.append(acc)
            for k in range(CAP):
                acc = None
                for X in range(4):
                    shift = (32 * (X - k)) % L
                    part = merged[X] if shift == 0 else pltpu.roll(merged[X], shift, 1)
                    acc = part if acc is None else jnp.where(ls == X, part, acc)
                dst[k] = acc

        ghost_messages(S[2:8, 2:8, 0], MO)
        fin_cp.wait()
        for t in range(4 * CAP):
            FT[t // 4, t % 4, 0:F, :] = FIN[:, t * L : (t + 1) * L]

        def fill1(o, buf):
            buf[o, 0:4] = FT[kf_s[o]]
            buf[o, 4] = MO[kg_s[o]]

        fill1(0, RB1)

        def send1(o, _):
            fill1(o, SB1)
            pltpu.make_async_remote_copy(
                src_ref=SB1.at[o],
                dst_ref=RB1.at[o],
                send_sem=m_send.at[0],
                recv_sem=m_recv.at[0],
                device_id=(a, lax.rem(b + o, n_gy)),
                device_id_type=MESH,
            ).start()
            return 0

        lax.fori_loop(1, n_gy, send1, 0)


        def cells(x, y, j):
            start = (((x + 2) * 10 + (y + 2)) * 3 + j) * 8
            return [take(S, start + f, 8, 24) for f in range(F)]

        for x in range(SIDE):
            for y in range(SIDE):
                WN[x, y] = jnp.where(lane < L - 2, S[x + 2, y + 2, 0], S[x + 2, y + 2, 2])
        for cp in halos[:4]:
            cp.wait_recv()

        slot24 = (lane >= 6).astype(jnp.int32) + (lane >= 12).astype(jnp.int32) + (lane >= 18).astype(jnp.int32)
        zpos = lane - 6 * slot24
        alive_lane = jnp.where(
            slot24 == 0, alive[0], jnp.where(slot24 == 1, alive[1], jnp.where(slot24 == 2, alive[2], alive[3]))
        )
        live_z = (lane < 24) & (alive_lane == 1)
        zin = live_z & (zpos >= 1) & (zpos <= 4)
        yin = (sub >= 1) & (sub <= 4)
        inner = yin & zin
        y_low, y_high = (sub == 0) & zin, (sub == 5) & zin
        z_low, z_high = yin & live_z & (zpos == 0), yin & live_z & (zpos == 5)

        def y_parts(x, j):
            plus, minus = split_flux(cells(x, -2, j), cells(x, -1, j), cells(x, 0, j), 1)
            g = [p + pltpu.roll(m, 7, 0) for p, m in zip(plus, minus)]
            return g, [pltpu.roll(v, 7, 0) for v in g]

        def z_circle(left_edge, mid, right_edge):
            um = [pltpu.roll(jnp.where(lane == L - 1, l, c), 1, 1) for l, c in zip(left_edge, mid)]
            up = [pltpu.roll(jnp.where(lane == 0, r, c), L - 1, 1) for r, c in zip(right_edge, mid)]
            return split_flux(um, mid, up, 2)

        def x_fluxes(j):
            faces = []
            before = None
            um, u = cells(-2, 0, j), cells(-1, 0, j)
            for x in range(-1, 7):
                up = cells(x + 1, 0, j)
                plus, minus = split_flux(um, u, up, 0)
                if before is not None:
                    faces.append([p + m for p, m in zip(before, minus)])
                before = plus
                um, u = u, up
                if len(faces) >= 2:
                    yield x - 1, faces[-2], faces[-1]

        for x, lower, upper in x_fluxes(0):
            u = cells(x, 0, 0)
            y_lo, y_up = y_parts(x, 0)
            circle = [take(WN, x * 64 + f, 8, 8) for f in range(F)]
            plus, minus = z_circle(circle, circle, circle)
            change, masked = [], []
            for f in range(F):
                g = plus[f] + pltpu.roll(minus[f], L - 1, 1)
                dz = g - pltpu.roll(g, 1, 1)
                dx = upper[f] - lower[f]
                dy = y_up[f] - y_lo[f]
                change.append(dx + dy + dz)
                if x == 0:
                    dxm = jnp.where(inner, 0.0, upper[f]) - lower[f]
                    dym = dy
                elif x == 5:
                    dxm = upper[f] - jnp.where(inner, 0.0, lower[f])
                    dym = dy
                else:
                    dxm = dx
                    dym = jnp.where(y_low, 0.0, y_up[f]) - jnp.where(y_high, 0.0, y_lo[f])
                masked.append(dxm + dym)
            new = react(u, change, 0.05)
            for f in range(F):
                put(NEWC, x * 64 + f, 8, 8, new[f])
                CM[x, f] = masked[f]

        ghost_messages(NEWC[:, 0:SIDE], MN)
        RB2[0] = MN[kg_s[0]]

        def send2(o, _):
            SB2[o] = MN[kg_s[o]]
            pltpu.make_async_remote_copy(
                src_ref=SB2.at[o],
                dst_ref=RB2.at[o],
                send_sem=m_send.at[1],
                recv_sem=m_recv.at[1],
                device_id=(a, lax.rem(b + o, n_gy)),
                device_id_type=MESH,
            ).start()
            return 0

        lax.fori_loop(1, n_gy, send2, 0)

        for cp in halos[4:]:
            cp.wait_recv()

        def z_parts(j, _):
            jm, jp = lax.rem(j + 2, 3), lax.rem(j + 1, 3)
            for x in range(SIDE):
                plus, minus = z_circle(cells(x, 0, jm), cells(x, 0, j), cells(x, 0, jp))
                for f in range(F):
                    PZ[j, x, f] = plus[f]
                    MZ[j, x, f] = minus[f]
            return 0

        lax.fori_loop(0, 3, z_parts, 0)

        def z_faces(x, f, j):
            jm, jp = lax.rem(j + 2, 3), lax.rem(j + 1, 3)
            p, m = PZ[j, x, f], MZ[j, x, f]
            upper = p + pltpu.roll(jnp.where(lane == 0, MZ[jp, x, f], m), L - 1, 1)
            lower = m + pltpu.roll(jnp.where(lane == L - 1, PZ[jm, x, f], p), 1, 1)
            return lower, upper

        def store(x, j, new):
            for f in range(F):
                put(BASE, (x * 24 + j) * 8 + f, 8, 24, new[f])

        zero = jnp.int32(0)
        for x in range(SIDE):
            change = []
            for f in range(F):
                lower, upper = z_faces(x, f, zero)
                if 1 <= x <= 4:
                    lower = jnp.where(z_high, 0.0, lower)
                    upper = jnp.where(z_low, 0.0, upper)
                change.append(CM[x, f] + (upper - lower))
            store(x, zero, react(cells(x, 0, 0), change, 0.05))

        def rest(j, _):
            for x, lower, upper in x_fluxes(j):
                y_lo, y_up = y_parts(x, j)
                change = []
                for f in range(F):
                    z_lo, z_up = z_faces(x, f, j)
                    change.append((upper[f] - lower[f]) + (y_up[f] - y_lo[f]) + (z_up - z_lo))
                store(x, j, react(cells(x, 0, j), change, 0.05))
            return 0

        lax.fori_loop(1, 3, rest, 0)

        def wait_messages(buf, i):
            whole = buf.at[1:n_gy]
            pltpu.make_async_copy(whole, whole, m_recv.at[i]).wait()

        my_src = [lax.rem(b + n_gy - src_s[k, b], n_gy) for k in range(CAP)]
        my_live = [live_s[k, b] for k in range(CAP)]

        def ghost_fields(messages):
            for k in range(2 * CAP):
                for X in range(4):
                    tile = messages[k]
                    GL[k, X] = tile if X == 0 else pltpu.roll(tile, L - 32 * X, 1)
            expanded = exact_dot(GL[...].reshape(2 * CAP * 32, L), EG[...])
            for i in range(3):
                GG[i] = expanded[:, i * L : (i + 1) * L]
            return [[GG[i, pl.ds(f, 8 * CAP, stride=8), :] for f in range(F)] for i in range(3)]

        wait_messages(RB1, 0)
        for k in range(CAP):
            FS[k] = RB1[owner[k], 0:4]
            FS[CAP + k] = FT[k]
        R = 8 * CAP
        flane = iota((R, L), 1)
        frow = iota((R, L), 0) & 3
        fz1, fy1, fxb = flane & 7, (flane >> 3) & 7, flane >> 6
        at_z0, at_z7 = fz1 == 0, fz1 == 7
        at_y0, at_y7 = fy1 == 0, fy1 == 7
        odd = fxb == 1
        first_row, last_row = frow == 0, frow == 3
        at_x0 = first_row & jnp.logical_not(odd)
        at_x7 = last_row & odd

        def lane_down(step):
            return lambda v: pltpu.roll(v, step, 1)

        def lane_up(step):
            return lambda v: pltpu.roll(v, L - step, 1)

        def x_down(v):
            r = pltpu.roll(v, 64, 1)
            return jnp.where(odd, r, pltpu.roll(r, 1, 0))

        def x_up(v):
            r = pltpu.roll(v, 64, 1)
            return jnp.where(odd, pltpu.roll(r, R - 1, 0), r)

        plan = (
            (2, 0, lane_down(1), lane_up(1), at_z0, at_z7, fz1 < 4),
            (1, 1, lane_down(8), lane_up(8), at_y0, at_y7, fy1 < 4),
            (0, 2, x_down, x_up, at_x0, at_x7, jnp.logical_not(odd)),
        )

        def substep(u, ghosts):
            change = None
            faces = []
            for d, gi, down, upw, at_lo, at_hi, lo_side in plan:
                g = ghosts[gi]
                um = [jnp.where(at_lo, w, down(c)) for c, w in zip(u, g)]
                up = [jnp.where(at_hi, w, upw(c)) for c, w in zip(u, g)]
                plus, minus = split_flux(um, u, up, d)
                sign = jnp.where(lo_side, 0.1, -0.1)
                edge = [h + sign * c for h, c in zip(half_flux(g, d), g)]
                lower, upper = [], []
                for f in range(F):
                    lower.append(minus[f] + jnp.where(at_lo, edge[f], down(plus[f])))
                    upper.append(plus[f] + jnp.where(at_hi, edge[f], upw(minus[f])))
                diff = [q - p for q, p in zip(upper, lower)]
                change = diff if change is None else [c + v for c, v in zip(change, diff)]
                faces.append(
                    [
                        jnp.where(at_lo[0:16], -p[0:16], jnp.where(at_hi[0:16], q[0:16], 0.0))
                        for q, p in zip(upper, lower)
                    ]
                )
            return react(u, change, 0.025), faces

        old = [MO[k] for k in range(CAP)] + [RB1[my_src[k], 4] for k in range(CAP)]
        u0 = [take(FS, f, R, 8) for f in range(F)]
        u1, faces1 = substep(u0, ghost_fields(old))
        for f in range(F):
            put(FS, f, R, 8, u1[f])
            for i in range(3):
                LW[1 + i, pl.ds(f, 16, stride=8), :] = faces1[i][f]

        wait_messages(RB2, 1)
        new = [MN[k] for k in range(CAP)] + [RB2[my_src[k]] for k in range(CAP)]
        old = [MO[k] for k in range(CAP)] + [RB1[my_src[k], 4] for k in range(CAP)]
        mean = [0.5 * (o + n) for o, n in zip(old, new)]
        u1 = [take(FS, f, R, 8) for f in range(F)]
        u2, faces2 = substep(u1, ghost_fields(mean))
        for f in range(F):
            put(FS, f, R, 8, u2[f])
            LW[0, pl.ds(f, 16, stride=8), :] = u2[f][0:16]
            for i in range(3):
                rows = pl.ds(f, 16, stride=8)
                LW[1 + i, rows, :] = LW[1 + i, rows, :] + faces2[i][f]

        for t in range(4 * CAP):
            k = t // 4
            fine_out[:, t * L : (t + 1) * L] = jnp.where(
                my_live[k] == 1, FS[CAP + k, t % 4, 0:F, :], FT[k, t % 4, 0:F, :]
            )

        TT[0] = exact_dot(jnp.concatenate([LW[0], LW[1], LW[2]], axis=1), WD[...])
        TT[1] = exact_dot(LW[3], WX[...])
        slot_live = jnp.where(ls == 0, alive[0], jnp.where(ls == 1, alive[1], jnp.where(ls == 2, alive[2], alive[3])))
        keep = slot_live == 1

        def by_slot(i, X):
            acc = TT[i, pl.ds(X * 8, 8), :]
            for k in range(1, CAP):
                acc = jnp.where(ls == k, TT[i, pl.ds((k * 4 + X) * 8, 8), :], acc)
            return jnp.where(keep, acc, 0.0)

        l6 = (lc * 43) >> 8
        lyv = jnp.where(lc < 24, l6 + 1, jnp.where(lc < 28, 0, 5))
        blocks = []
        for X in range(4):
            t = by_slot(0, X)
            for y in range(6):
                blocks.append(jnp.where(lyv == y, t, 0.0))
        inside = exact_dot(jnp.concatenate(blocks, axis=0), E2[...])
        lxy = (lc >> 2) + 1
        blocks = []
        for X in (0, 3):
            t = by_slot(1, X)
            for y in range(1, 5):
                blocks.append(jnp.where(lxy == y, t, 0.0))
        across = exact_dot(jnp.concatenate(blocks, axis=0), E2X[...])
        for x in range(SIDE):
            for y in range(SIDE):
                tile = BASE[x, y, 0]
                if 1 <= x <= 4:
                    i = ((x - 1) * 6 + y) * 8
                    part = inside[i : i + 8]
                    if 1 <= y <= 4:
                        tile = jnp.where(zin, part, tile + part)
                    else:
                        tile = tile + part
                elif 1 <= y <= 4:
                    i = ((0 if x == 0 else 4) + y - 1) * 8
                    tile = tile + across[i : i + 8]
                coarse_out[x, y, :, 0:L] = tile[0:F]
                for j in (1, 2):
                    coarse_out[x, y, :, j * L : (j + 1) * L] = BASE[x, y, j, 0:F]

        for cp in halos:
            cp.wait_send()
        for i, buf in enumerate((SB1, SB2)):
            whole = buf.at[1:n_gy]
            pltpu.make_async_copy(whole, whole, m_send.at[i]).wait()

    return kernel


def solution(mesh):
    n_gx, n_gy = mesh.shape["gx"], mesh.shape["gy"]
    kernel = make_kernel(n_gx, n_gy)

    def local(coarse_state, fine_state, patch_source, patch_live):
        coarse = jnp.transpose(coarse_state, (1, 2, 0, 3))
        source = jnp.transpose(patch_source, (0, 2, 1))
        live = jnp.transpose(patch_live, (0, 2, 1))
        v = pltpu.VMEM
        anywhere = pl.BlockSpec(memory_space=pl.ANY)
        vmem = pl.BlockSpec(memory_space=pltpu.VMEM)
        coarse_out, fine_out = pl.pallas_call(
            kernel,
            out_shape=(
                jax.ShapeDtypeStruct(coarse.shape, F32),
                jax.ShapeDtypeStruct(fine_state.shape, F32),
            ),
            in_specs=[anywhere] * 4,
            out_specs=(vmem, vmem),
            scratch_shapes=[
                v((10, 10, 3, 8, L), F32),
                v((F, 4 * CAP * L), F32),
                v((SIDE, 8, 3, 8, L), F32),
                v((SIDE, 8, 8, L), F32),
                v((SIDE, 8, 8, L), F32),
                v((3, SIDE, F, 8, L), F32),
                v((3, SIDE, F, 8, L), F32),
                v((SIDE, F, 8, L), F32),
                v((SIDE, SIDE, 8, L), F32),
                v((CAP, 8, L), F32),
                v((CAP, 8, L), F32),
                v((2 * CAP, 4, 8, L), F32),
                v((2 * CAP, 4, 8, L), F32),
                v((CAP, 4, 8, L), F32),
                v((3, 2 * CAP * 32, L), F32),
                v((n_gy, 5, 8, L), F32),
                v((n_gy, 5, 8, L), F32),
                v((n_gy, 8, L), F32),
                v((n_gy, 8, L), F32),
                v((L, L), BF16),
                v((L, 3 * L), BF16),
                v((3 * L, L), BF16),
                v((L, L), BF16),
                v((L, L), BF16),
                v((L, L), BF16),
                v((4, CAP * 32, L), F32),
                v((2, CAP * 32, L), F32),
                pltpu.SMEM((CAP, n_gy), jnp.int32),
                pltpu.SMEM((CAP, n_gy), jnp.int32),
                pltpu.SMEM((n_gy,), jnp.int32),
                pltpu.SMEM((n_gy,), jnp.int32),
                pltpu.SemaphoreType.DMA((3,)),
                pltpu.SemaphoreType.DMA,
                pltpu.SemaphoreType.DMA((2,)),
                pltpu.SemaphoreType.DMA((3, 4)),
                pltpu.SemaphoreType.DMA((3, 4)),
                pltpu.SemaphoreType.DMA((2,)),
                pltpu.SemaphoreType.DMA((2,)),
            ],
            compiler_params=pltpu.CompilerParams(
                collective_id=0, has_side_effects=True, vmem_limit_bytes=48 * 2**20
            ),
        )(coarse, fine_state, source, live)
        return jnp.transpose(coarse_out, (2, 0, 1, 3)), fine_out

    return jax.shard_map(
        local,
        mesh=mesh,
        in_specs=(P(None, "gx", "gy", None), P(None, ("gx", "gy")), P(), P()),
        out_specs=(P(None, "gx", "gy", None), P(None, ("gx", "gy"))),
        check_vma=False,
    )
```

time: 503 us -> 30.8 us (0.06); the launches traced: 496 us -> 30.5 us
  local copies, waits for them, and re-layouts: 376 us -> 4.75 us
  other arithmetic: 64.6 us -> 0 us
  starting transfers between devices: 33.9 us -> 0 us
  Pallas kernels: 0 us -> 25.1 us
  waiting for transfers between devices: 14.1 us -> 0 us
  matrix products: 5.06 us -> 0 us
    scatter x6 -> x0, local copies, waits for them, and re-layouts: 157 us -> none  [the longest x4 155 us: fill_block(): spread = spread.at[:, 2:-2, 2:-2, :, 2:-2].set(interior)]
    reshape x20 -> x0, local copies, waits for them, and re-layouts: 89.5 us -> none  [the longest x1 14 us: local(): flux_y.reshape(FIELDS, coarse_side, coarse_side + 1, zslots, coarse_side)]
    slice x34 -> x0, local copies, waits for them, and re-layouts: 46.9 us -> none  [the longest x4 10 us: fine_substep(): along_z[..., -1]]
    all_to_all x4 -> x0, starting transfers between devices: 26.3 us -> none  [the longest x1 9.74 us: local(): lax.all_to_all(sent_old, 'gy', split_axis=0, concat_axis=0, tiled=True)]
    pallas_call x0 -> x1, Pallas kernels: none -> 25.1 us  [local(): pl.pallas_call(kernel, out_shape=(jax.ShapeDtypeStruct(coarse.shape, F32)...]
    unnamed x128 -> x10, local copies, waits for them, and re-layouts: 28.4 us -> 4.75 us
    mul x37 -> x0, other arithmetic: 20.1 us -> none  [the longest x12 8.76 us: euler_flux(): rows_out.append((fields[4] + pressure) * velocity)]
    another operation x17 -> x0, local copies, waits for them, and re-layouts: 19.1 us -> none  [the longest x12 19.1 us: euler_flux(): return jnp.stack(rows_out)]
  transfers between devices with their start and end apart: 8 -> 0, of which waited for: 3 -> 0; matrix products, arithmetic and copies ran while one was open for 13% -> 0% of each run, Pallas kernels for 0% -> 0%
where the time goes in v1:
time: 30.8 us; the launch traced here: 30.5 us
  Pallas kernels  25.1 us (81%)
  local copies, waits for them, and re-layouts  4.75 us (15%)
  between operations  0.65 us (2%)
    pallas_call x1, Pallas kernels, local(): pl.pallas_call(kernel, out_shape=(jax.ShapeDtypeStruct(coarse.shape, F32)...  25.1 us
    unnamed x10, local copies, waits for them, and re-layouts  4.75 us

profile of v1, /device:TPU:1, one launch (start us, length us, event | category | flops | bytes accessed | tf_op | source)
XLA Modules:
  0.0 30.5 jit_solution(14737021686010653454)
XLA Ops:
  0.6 0.0 copy-start
  0.6 1.0 %copy-done = f32[7,6,6,384]{3,0,2,1:T(8,128)S(1)} copy-done((f32[7,6,6,384]{3,0,2,1:T(8,128)S(1)}, f32[7,6,6,384]{3,0,2,1:T(8,128)}, u32[]{:S(2)}) %copy-start) | copy-done | bytes 387096
  1.6 0.0 copy-start.1
  1.6 0.8 %copy-done.1 = f32[7,2048]{1,0:T(8,128)S(1)} copy-done((f32[7,2048]{1,0:T(8,128)S(1)}, f32[7,2048]{1,0:T(8,128)}, u32[]{:S(2)}) %copy-start.1) | copy-done | bytes 57368
  2.5 0.0 copy-start.2
  2.5 0.8 %copy-done.2 = s32[16,16,4]{1,2,0:T(4,128)S(1)} copy-done((s32[16,16,4]{1,2,0:T(4,128)S(1)}, s32[16,16,4]{1,2,0:T(4,128)}, u32[]{:S(2)}) %copy-start.2) | copy-done | bytes 4120
  3.2 0.0 copy-start.3
  3.2 0.8 %copy-done.3 = s32[16,16,4]{1,2,0:T(4,128)S(1)} copy-done((s32[16,16,4]{1,2,0:T(4,128)S(1)}, s32[16,16,4]{1,2,0:T(4,128)}, u32[]{:S(2)}) %copy-start.3) | copy-done | bytes 4120
  4.0 25.1 %shard_map.59 = (f32[6,6,7,384]{3,2,1,0:T(8,128)S(1)}, f32[7,2048]{1,0:T(8,128)S(1)}) custom-call(f32[6,6,7,384]{3,2,1,0:T(8,128)S(1)} %bitcast.5, f32[7,2048]{1,0:T(8,128)S(1)} %copy-done.1, s32[16,4,16]{2,1,0:T(4,128)S(1)} %bitcast.6, s32[16,4,16]{2,1,0:T(4,128)S(1)} %bitcast.7), custom_call_target="tpu_custom_call" | custom-call | tf_op jit(solution)/shard_map/pallas_call | solution.py:566
  29.1 0.8 %copy.8 = f32[7,6,6,384]{3,0,2,1:T(8,128)} copy(f32[7,6,6,384]{3,0,2,1:T(8,128)S(1)} %bitcast.4) | data formatting | bytes 774144
  29.9 0.6 %copy.9 = f32[7,2048]{1,0:T(8,128)} copy(f32[7,2048]{1,0:T(8,128)S(1)} %get-tuple-element.9) | data formatting | bytes 114688
Async XLA Ops:
  0.6 1.0 %copy-start = (f32[7,6,6,384]{3,0,2,1:T(8,128)S(1)}, f32[7,6,6,384]{3,0,2,1:T(8,128)}, u32[]{:S(2)}) copy-start(f32[7,6,6,384]{3,0,2,1:T(8,128)} %param.4) | copy-start | bytes 1161220
  1.6 0.8 %copy-start.1 = (f32[7,2048]{1,0:T(8,128)S(1)}, f32[7,2048]{1,0:T(8,128)}, u32[]{:S(2)}) copy-start(f32[7,2048]{1,0:T(8,128)} %fine.1) | copy-start | bytes 172036
  2.5 0.8 %copy-start.2 = (s32[16,16,4]{1,2,0:T(4,128)S(1)}, s32[16,16,4]{1,2,0:T(4,128)}, u32[]{:S(2)}) copy-start(s32[16,16,4]{1,2,0:T(4,128)} %param.6) | copy-start | bytes 12292
  3.2 0.8 %copy-start.3 = (s32[16,16,4]{1,2,0:T(4,128)S(1)}, s32[16,16,4]{1,2,0:T(4,128)}, u32[]{:S(2)}) copy-start(s32[16,16,4]{1,2,0:T(4,128)} %param.7) | copy-start | bytes 12292

commit v2 on v1

v2 whole, which is shorter than its diff:
```python
import jax
import jax.numpy as jnp
from jax import lax
from jax.experimental import pallas as pl
from jax.experimental.pallas import tpu as pltpu
from jax.sharding import PartitionSpec as P

F = 7
CAP = 4
SIDE = 6
L = 128
F32 = jnp.float32
BF16 = jnp.bfloat16
MESH = pl.DeviceIdType.MESH


def iota(shape, dim):
    return lax.broadcasted_iota(jnp.int32, shape, dim)


def take(ref, start, count, stride):
    return ref.reshape(ref.size // L, L)[pl.ds(start, count, stride=stride), :]


def put(ref, start, count, stride, value):
    ref.reshape(ref.size // L, L)[pl.ds(start, count, stride=stride), :] = value


def exact_dot(a, e):
    hi = a.astype(BF16)
    rest = a - hi.astype(F32)
    mid = rest.astype(BF16)
    low = (rest - mid.astype(F32)).astype(BF16)
    out = jnp.dot(hi, e, preferred_element_type=F32)
    out = out + jnp.dot(mid, e, preferred_element_type=F32)
    return out + jnp.dot(low, e, preferred_element_type=F32)


def minmod(a, b):
    return jnp.maximum(jnp.minimum(a, b), 0.0) + jnp.minimum(jnp.maximum(a, b), 0.0)


def half_flux(u, d):
    inv = 1.0 / u[0]
    kk = u[1] * u[1] + u[2] * u[2] + u[3] * u[3]
    p = 0.4 * u[4] - 0.2 * (kk * inv)
    scaled = 0.025 * u[1 + d]
    v = scaled * inv
    out = [scaled]
    for i in range(3):
        term = u[1 + i] * v
        if i == d:
            term = term + 0.025 * p
        out.append(term)
    out += [(u[4] + p) * v, u[5] * v, u[6] * v]
    return out


def split_flux(um, u, up, d):
    h = [0.5 * minmod(c - m, q - c) for m, c, q in zip(um, u, up)]
    left = [c + s for c, s in zip(u, h)]
    right = [c - s for c, s in zip(u, h)]
    plus = [f + 0.1 * c for f, c in zip(half_flux(left, d), left)]
    minus = [f - 0.1 * c for f, c in zip(half_flux(right, d), right)]
    return plus, minus


def react(u, change, t):
    burned = (10.0 * t) * u[5]
    new = [c - g for c, g in zip(u, change)]
    new[4] = new[4] + 2.0 * burned
    new[5] = new[5] - burned
    new[6] = new[6] + burned
    return new


def make_kernel(n_gx, n_gy):
    def kernel(
        coarse, fine, source, live, coarse_out, fine_out,
        S, OWN, FIN, BASE, NEWC, PZ, MZ, PX, MX, CH, CM, BB, MO, MN, GL, FS, FT, GG, SB1, RB1, SB2, RB2,
        EZ, EG, WD, WX, E2, E2X, LW, TT, src_s, live_s, kf_s, kg_s,
        in_sem, fin_sem, tab_sem, h_send, h_recv, m_send, m_recv,
    ):
        a = lax.axis_index("gx")
        b = lax.axis_index("gy")
        up_a, dn_a = lax.rem(a + 1, n_gx), lax.rem(a + n_gx - 1, n_gx)
        up_b, dn_b = lax.rem(b + 1, n_gy), lax.rem(b + n_gy - 1, n_gy)

        barrier = pltpu.get_barrier_semaphore()
        for d in (up_a, dn_a):
            pl.semaphore_signal(barrier, inc=1, device_id=(d, b), device_id_type=MESH)

        def partner(i):
            half = lax.div(i + 1, 2)
            return n_gy // 2 + jnp.where(lax.rem(i, 2) == 1, half, -half)

        def greet(i, _):
            pl.semaphore_signal(
                barrier, inc=1, device_id=(a, lax.rem(b + partner(i), n_gy)), device_id_type=MESH
            )
            return 0

        lax.fori_loop(0, n_gy - 1, greet, 0)

        own = []
        for j in range(3):
            lanes = pl.ds(j * L, L)
            own.append(pltpu.make_async_copy(coarse.at[:, :, :, lanes], OWN.at[2:8, 0:SIDE, j, 0:F, :], in_sem.at[0, j]))
        for j in range(3):
            lanes = pl.ds(j * L, L)
            own.append(pltpu.make_async_copy(coarse.at[:, :, :, lanes], S.at[:, 2:8, j, 0:F, :], in_sem.at[1, j]))
        fin_cp = pltpu.make_async_copy(fine, FIN, fin_sem)
        tabs = [
            pltpu.make_async_copy(source.at[a], src_s, tab_sem.at[0]),
            pltpu.make_async_copy(live.at[a], live_s, tab_sem.at[1]),
        ]
        for cp in tabs + own[:1] + [fin_cp] + own[1:]:
            cp.start()

        row = iota((L, L), 0)
        col = iota((L, L), 1)
        c32 = col & 31
        s32 = col >> 5
        zc = jnp.where(
            c32 < 4, 0, jnp.where(c32 < 8, 5, jnp.where(c32 < 12, c32 - 7, jnp.where(c32 < 16, c32 - 11, (c32 & 3) + 1)))
        )
        EZ[...] = (row == 6 * s32 + zc).astype(F32).astype(BF16)
        fy = (col >> 3) & 7
        fz = col & 7
        cz, cy = fz >> 1, fy >> 1
        EG[:, 0:L] = (row == jnp.where(fz < 4, 0, 4) + cy).astype(F32).astype(BF16)
        EG[:, L : 2 * L] = (row == jnp.where(fy < 4, 8, 12) + cz).astype(F32).astype(BF16)
        EG[:, 2 * L : 3 * L] = (row == 16 + cy * 4 + cz).astype(F32).astype(BF16)

        for cp in tabs:
            cp.wait()

        def route(o, carry):
            owner, alive = carry
            d = lax.rem(b + o, n_gy)
            kf = jnp.int32(0)
            kg = jnp.int32(0)
            back = lax.rem(n_gy - o, n_gy)
            own_new, live_new = [], []
            for k in reversed(range(CAP)):
                kf = jnp.where((src_s[k, b] == d) & (live_s[k, b] == 1), k, kf)
                mine = src_s[k, d] == b
                lv = live_s[k, d]
                kg = jnp.where(mine & (lv == 1), k, kg)
                own_new.append(jnp.where(mine, back, owner[k]))
                live_new.append(jnp.where(mine, lv, alive[k]))
            kf_s[o] = kf
            kg_s[o] = kg
            return tuple(reversed(own_new)), tuple(reversed(live_new))

        zeros = (jnp.int32(0),) * CAP
        owner, alive = lax.fori_loop(0, n_gy, route, (zeros, zeros))

        lane = iota((8, L), 1)
        sub = iota((8, L), 0)
        lc = lane & 31
        ls = lane >> 5
        ly = jnp.where(
            lc < 4, lc + 1, jnp.where(lc < 8, lc - 3, jnp.where(lc < 12, 0, jnp.where(lc < 16, 5, ((lc - 16) >> 2) + 1)))
        )
        low16 = lc < 16

        def ghost_messages(tiles, dst):
            BB[...] = exact_dot(tiles.reshape(SIDE * SIDE * 8, L), EZ[...]).reshape(SIDE, SIDE, 8, L)
            merged = []
            for X in range(4):
                acc = BB[X + 1, 0]
                for y in range(1, 6):
                    acc = jnp.where(low16 & (ly == y), BB[X + 1, y], acc)
                if X in (0, 3):
                    for y in range(1, 5):
                        acc = jnp.where(
                            jnp.logical_not(low16) & (ly == y), BB[0 if X == 0 else 5, y], acc
                        )
                merged.append(acc)
            for k in range(CAP):
                acc = None
                for X in range(4):
                    shift = (32 * (X - k)) % L
                    part = merged[X] if shift == 0 else pltpu.roll(merged[X], shift, 1)
                    acc = part if acc is None else jnp.where(ls == X, part, acc)
                dst[k] = acc

        own[0].wait()
        ghost_messages(OWN[2:8, 0:SIDE, 0], MO)
        fin_cp.wait()
        for t in range(4 * CAP):
            FT[t // 4, t % 4, 0:F, :] = FIN[:, t * L : (t + 1) * L]

        def fill1(o, buf):
            buf[o, 0:4] = FT[kf_s[o]]
            buf[o, 4] = MO[kg_s[o]]

        fill1(0, RB1)

        def fill(o, _):
            fill1(o, SB1)
            return 0

        lax.fori_loop(1, n_gy, fill, 0)
        for cp in own[1:]:
            cp.wait()
        pl.semaphore_wait(barrier, n_gy + 1)

        def halo(j):
            copies = []
            for h, (buf, src, dst, dev) in enumerate(
                (
                    (OWN, OWN.at[6:8, 0:SIDE, j, 0:F, :], OWN.at[0:2, 0:SIDE, j, 0:F, :], (up_a, b)),
                    (OWN, OWN.at[2:4, 0:SIDE, j, 0:F, :], OWN.at[8:10, 0:SIDE, j, 0:F, :], (dn_a, b)),
                    (S, S.at[:, 6:8, j, 0:F, :], S.at[:, 0:2, j, 0:F, :], (a, up_b)),
                    (S, S.at[:, 2:4, j, 0:F, :], S.at[:, 8:10, j, 0:F, :], (a, dn_b)),
                )
            ):
                cp = pltpu.make_async_remote_copy(
                    src_ref=src,
                    dst_ref=dst,
                    send_sem=h_send.at[j, h],
                    recv_sem=h_recv.at[j, h],
                    device_id=dev,
                    device_id_type=MESH,
                )
                cp.start()
                copies.append(cp)
            return copies

        halos = halo(0)

        def send1(i, _):
            o = partner(i)
            pltpu.make_async_remote_copy(
                src_ref=SB1.at[o, :, 0:F, :],
                dst_ref=RB1.at[o, :, 0:F, :],
                send_sem=m_send.at[0],
                recv_sem=m_recv.at[0],
                device_id=(a, lax.rem(b + o, n_gy)),
                device_id_type=MESH,
            ).start()
            return 0

        lax.fori_loop(0, n_gy - 1, send1, 0)
        halos += halo(1) + halo(2)

        def cells(x, j):
            start = ((x + 2) * 24 + j) * 8
            return [take(OWN, start + f, 8, 24) for f in range(F)]

        def y_cells(x, y, j):
            start = ((x * 10 + y + 2) * 3 + j) * 8
            return [take(S, start + f, 8, 24) for f in range(F)]

        def x_split(x, j):
            return split_flux(cells(x - 1, j), cells(x, j), cells(x + 1, j), 0)

        def z_parts(j, _):
            jm, jp = lax.rem(j + 2, 3), lax.rem(j + 1, 3)
            for x in range(SIDE):
                mid = cells(x, j)
                um = [pltpu.roll(jnp.where(lane == L - 1, l, c), 1, 1) for l, c in zip(cells(x, jm), mid)]
                up = [pltpu.roll(jnp.where(lane == 0, r, c), L - 1, 1) for r, c in zip(cells(x, jp), mid)]
                plus, minus = split_flux(um, mid, up, 2)
                for f in range(F):
                    PZ[j, x, f] = plus[f]
                    MZ[j, x, f] = minus[f]
            return 0

        lax.fori_loop(0, 3, z_parts, 0)
        for x in range(1, 5):
            plus, minus = x_split(x, 0)
            for f in range(F):
                PX[x, f] = plus[f]
                MX[x, f] = minus[f]

        ry = (row >> 3) & 7
        rz = row & 7
        rzc, ryc = rz >> 1, ry >> 1
        e6 = (c32 * 43) >> 8
        eyv = jnp.where(c32 < 24, e6 + 1, jnp.where(c32 < 28, 0, 5))
        ezv = jnp.where(c32 < 24, c32 - 6 * e6, (c32 & 3) + 1)
        main = c32 < 24
        wa = main & (ezv >= 1) & (ezv <= 4) & (ryc == eyv - 1) & (rzc == ezv - 1)
        wz = main & (ryc == eyv - 1) & (((ezv == 0) & (rz == 0)) | ((ezv == 5) & (rz == 7)))
        wy = (
            jnp.logical_not(main)
            & (rzc == ezv - 1)
            & (((eyv == 0) & (ry == 0)) | ((eyv == 5) & (ry == 7)))
        )
        for i, w in enumerate((wa, wz, wy)):
            WD[i * L : (i + 1) * L, :] = jnp.where(w, 0.125, 0.0).astype(BF16)
        WX[...] = jnp.where((ryc == (c32 >> 2)) & (rzc == (c32 & 3)), 0.125, 0.0).astype(BF16)
        r32 = row & 31
        rs = row >> 5
        r6 = (r32 * 43) >> 8
        rzv = jnp.where(r32 < 24, r32 - 6 * r6, (r32 & 3) + 1)
        E2[...] = (col == 6 * rs + rzv).astype(F32).astype(BF16)
        E2X[...] = (col == 6 * rs + (r32 & 3) + 1).astype(F32).astype(BF16)

        slot24 = (lane >= 6).astype(jnp.int32) + (lane >= 12).astype(jnp.int32) + (lane >= 18).astype(jnp.int32)
        zpos = lane - 6 * slot24
        alive_lane = jnp.where(
            slot24 == 0, alive[0], jnp.where(slot24 == 1, alive[1], jnp.where(slot24 == 2, alive[2], alive[3]))
        )
        live_z = (lane < 24) & (alive_lane == 1)
        zin = live_z & (zpos >= 1) & (zpos <= 4)
        yin = (sub >= 1) & (sub <= 4)
        inner = yin & zin
        y_low, y_high = (sub == 0) & zin, (sub == 5) & zin
        z_low, z_high = yin & live_z & (zpos == 0), yin & live_z & (zpos == 5)

        def y_parts(x, j):
            plus, minus = split_flux(y_cells(x, -2, j), y_cells(x, -1, j), y_cells(x, 0, j), 1)
            g = [p + pltpu.roll(m, 7, 0) for p, m in zip(plus, minus)]
            return g, [pltpu.roll(v, 7, 0) for v in g]

        def z_faces(x, f, j):
            jm, jp = lax.rem(j + 2, 3), lax.rem(j + 1, 3)
            p, m = PZ[j, x, f], MZ[j, x, f]
            upper = p + pltpu.roll(jnp.where(lane == 0, MZ[jp, x, f], m), L - 1, 1)
            lower = m + pltpu.roll(jnp.where(lane == L - 1, PZ[jm, x, f], p), 1, 1)
            return lower, upper

        def store(x, j, new):
            for f in range(F):
                put(BASE, (x * 24 + j) * 8 + f, 8, 24, new[f])

        zero = jnp.int32(0)
        halos[2].wait_recv()
        halos[3].wait_recv()
        for x in range(SIDE):
            y_lo, y_up = y_parts(x, 0)
            for f in range(F):
                z_lo, z_up = z_faces(x, f, zero)
                whole = (y_up[f] - y_lo[f]) + (z_up - z_lo)
                CH[x, f] = whole
                if 1 <= x <= 4:
                    whole = (jnp.where(y_low, 0.0, y_up[f]) - jnp.where(y_high, 0.0, y_lo[f])) + (
                        jnp.where(z_low, 0.0, z_up) - jnp.where(z_high, 0.0, z_lo)
                    )
                CM[x, f] = whole
        halos[0].wait_recv()
        halos[1].wait_recv()
        ends = {x: x_split(x, 0) for x in (-1, 0, 5, 6)}

        def plus_of(x, f):
            return ends[x][0][f] if x in ends else PX[x, f]

        def minus_of(x, f):
            return ends[x][1][f] if x in ends else MX[x, f]

        lower = [plus_of(-1, f) + minus_of(0, f) for f in range(F)]
        for x in range(SIDE):
            upper = [plus_of(x, f) + minus_of(x + 1, f) for f in range(F)]
            new = react(cells(x, 0), [CH[x, f] + (upper[f] - lower[f]) for f in range(F)], 0.05)
            for f in range(F):
                put(NEWC, x * 64 + f, 8, 8, new[f])
                up_m, lo_m = upper[f], lower[f]
                if x == 0:
                    up_m = jnp.where(inner, 0.0, up_m)
                elif x == 5:
                    lo_m = jnp.where(inner, 0.0, lo_m)
                CM[x, f] = CM[x, f] + (up_m - lo_m)
            lower = upper

        ghost_messages(NEWC[:, 0:SIDE], MN)
        RB2[0] = MN[kg_s[0]]

        def send2(i, _):
            o = partner(i)
            SB2[o] = MN[kg_s[o]]
            pltpu.make_async_remote_copy(
                src_ref=SB2.at[o, 0:F, :],
                dst_ref=RB2.at[o, 0:F, :],
                send_sem=m_send.at[1],
                recv_sem=m_recv.at[1],
                device_id=(a, lax.rem(b + o, n_gy)),
                device_id_type=MESH,
            ).start()
            return 0

        lax.fori_loop(0, n_gy - 1, send2, 0)

        for x in range(SIDE):
            store(x, zero, react(cells(x, 0), [CM[x, f] for f in range(F)], 0.05))
        for cp in halos[4:]:
            cp.wait_recv()

        def rest(j, _):
            before = x_split(-1, j)[0]
            lower = None
            for x in range(SIDE + 1):
                plus, minus = x_split(x, j)
                upper = [p + m for p, m in zip(before, minus)]
                if lower is not None:
                    y_lo, y_up = y_parts(x - 1, j)
                    change = []
                    for f in range(F):
                        z_lo, z_up = z_faces(x - 1, f, j)
                        change.append((upper[f] - lower[f]) + (y_up[f] - y_lo[f]) + (z_up - z_lo))
                    store(x - 1, j, react(cells(x - 1, j), change, 0.05))
                before, lower = plus, upper
            return 0

        lax.fori_loop(1, 3, rest, 0)
        for x in range(SIDE):
            for y in range(SIDE):
                for j in (1, 2):
                    coarse_out[x, y, :, j * L : (j + 1) * L] = BASE[x, y, j, 0:F]

        def wait_messages(whole, sem):
            pltpu.make_async_copy(whole, whole, sem).wait()

        my_src = [lax.rem(b + n_gy - src_s[k, b], n_gy) for k in range(CAP)]
        my_live = [live_s[k, b] for k in range(CAP)]

        def ghost_fields(messages):
            n = len(messages)
            for k in range(n):
                for X in range(4):
                    tile = messages[k]
                    GL[k, X] = tile if X == 0 else pltpu.roll(tile, L - 32 * X, 1)
            expanded = exact_dot(GL[0:n].reshape(n * 32, L), EG[...])
            for i in range(3):
                GG[i, 0 : n * 32] = expanded[:, i * L : (i + 1) * L]
            return [[GG[i, pl.ds(f, 4 * n, stride=8), :] for f in range(F)] for i in range(3)]

        def lane_down(step):
            return lambda v: pltpu.roll(v, step, 1)

        def lane_up(step):
            return lambda v: pltpu.roll(v, L - step, 1)

        def substep(u, ghosts):
            R = u[0].shape[0]
            flane = iota((R, L), 1)
            frow = iota((R, L), 0) & 3
            z, y, odd = flane & 7, (flane >> 3) & 7, (flane >> 6) == 1
            even = jnp.logical_not(odd)

            def x_down(v):
                r = pltpu.roll(v, 64, 1)
                return jnp.where(odd, r, pltpu.roll(r, 1, 0))

            def x_up(v):
                r = pltpu.roll(v, 64, 1)
                return jnp.where(odd, pltpu.roll(r, R - 1, 0), r)

            plan = (
                (2, 0, lane_down(1), lane_up(1), z == 0, z == 7, z < 4),
                (1, 1, lane_down(8), lane_up(8), y == 0, y == 7, y < 4),
                (0, 2, x_down, x_up, (frow == 0) & even, (frow == 3) & odd, even),
            )
            change = None
            faces = []
            for d, gi, down, upw, at_lo, at_hi, lo_side in plan:
                g = ghosts[gi]
                um = [jnp.where(at_lo, w, down(c)) for c, w in zip(u, g)]
                up = [jnp.where(at_hi, w, upw(c)) for c, w in zip(u, g)]
                plus, minus = split_flux(um, u, up, d)
                sign = jnp.where(lo_side, 0.1, -0.1)
                edge = [h + sign * c for h, c in zip(half_flux(g, d), g)]
                lower, upper = [], []
                for f in range(F):
                    lower.append(minus[f] + jnp.where(at_lo, edge[f], down(plus[f])))
                    upper.append(plus[f] + jnp.where(at_hi, edge[f], upw(minus[f])))
                diff = [q - p for q, p in zip(upper, lower)]
                change = diff if change is None else [c + v for c, v in zip(change, diff)]
                faces.append(
                    [
                        jnp.where(at_lo[0:16], -p[0:16], jnp.where(at_hi[0:16], q[0:16], 0.0))
                        for q, p in zip(upper, lower)
                    ]
                )
            return react(u, change, 0.025), faces

        wait_messages(RB1.at[1:n_gy, :, 0:F, :], m_recv.at[0])
        for k in range(CAP):
            FS[k] = RB1[owner[k], 0:4]
            FS[CAP + k] = FT[k]
        old = [MO[k] for k in range(CAP)] + [RB1[my_src[k], 4] for k in range(CAP)]
        u0 = [take(FS, f, 8 * CAP, 8) for f in range(F)]
        u1, faces1 = substep(u0, ghost_fields(old))
        for f in range(F):
            put(FS, f, 8 * CAP, 8, u1[f])
            for i in range(3):
                LW[1 + i, pl.ds(f, 16, stride=8), :] = faces1[i][f]

        mean = [0.5 * (MO[k] + MN[k]) for k in range(CAP)]
        u1 = [take(FS, f, 16, 8) for f in range(F)]
        u2, faces2 = substep(u1, ghost_fields(mean))
        for f in range(F):
            rows = pl.ds(f, 16, stride=8)
            LW[0, rows, :] = u2[f]
            for i in range(3):
                LW[1 + i, rows, :] = LW[1 + i, rows, :] + faces2[i][f]

        TT[0] = exact_dot(jnp.concatenate([LW[0], LW[1], LW[2]], axis=1), WD[...])
        TT[1] = exact_dot(LW[3], WX[...])
        slot_live = jnp.where(ls == 0, alive[0], jnp.where(ls == 1, alive[1], jnp.where(ls == 2, alive[2], alive[3])))
        keep = slot_live == 1

        def by_slot(i, X):
            acc = TT[i, pl.ds(X * 8, 8), :]
            for k in range(1, CAP):
                acc = jnp.where(ls == k, TT[i, pl.ds((k * 4 + X) * 8, 8), :], acc)
            return jnp.where(keep, acc, 0.0)

        l6 = (lc * 43) >> 8
        lyv = jnp.where(lc < 24, l6 + 1, jnp.where(lc < 28, 0, 5))
        blocks = []
        for X in range(4):
            t = by_slot(0, X)
            for y in range(6):
                blocks.append(jnp.where(lyv == y, t, 0.0))
        inside = exact_dot(jnp.concatenate(blocks, axis=0), E2[...])
        lxy = (lc >> 2) + 1
        blocks = []
        for X in (0, 3):
            t = by_slot(1, X)
            for y in range(1, 5):
                blocks.append(jnp.where(lxy == y, t, 0.0))
        across = exact_dot(jnp.concatenate(blocks, axis=0), E2X[...])
        for x in range(SIDE):
            for y in range(SIDE):
                tile = BASE[x, y, 0]
                if 1 <= x <= 4:
                    i = ((x - 1) * 6 + y) * 8
                    part = inside[i : i + 8]
                    if 1 <= y <= 4:
                        tile = jnp.where(zin, part, tile + part)
                    else:
                        tile = tile + part
                elif 1 <= y <= 4:
                    i = ((0 if x == 0 else 4) + y - 1) * 8
                    tile = tile + across[i : i + 8]
                coarse_out[x, y, :, 0:L] = tile[0:F]

        wait_messages(RB2.at[1:n_gy, 0:F, :], m_recv.at[1])
        mean = [0.5 * (RB1[my_src[k], 4] + RB2[my_src[k]]) for k in range(CAP)]
        u1 = [take(FS, CAP * 32 + f, 16, 8) for f in range(F)]
        u2, _ = substep(u1, ghost_fields(mean))
        for f in range(F):
            put(FS, CAP * 32 + f, 16, 8, u2[f])
        for t in range(4 * CAP):
            k = t // 4
            fine_out[:, t * L : (t + 1) * L] = jnp.where(
                my_live[k] == 1, FS[CAP + k, t % 4, 0:F, :], FT[k, t % 4, 0:F, :]
            )

        for cp in halos:
            cp.wait_send()
        wait_messages(SB1.at[1:n_gy, :, 0:F, :], m_send.at[0])
        wait_messages(SB2.at[1:n_gy, 0:F, :], m_send.at[1])

    return kernel


def hand_over(coarse, fine, coarse_out, fine_out, sem):
    copies = [
        pltpu.make_async_copy(coarse, coarse_out, sem.at[0]),
        pltpu.make_async_copy(fine, fine_out, sem.at[1]),
    ]
    for cp in copies:
        cp.start()
    for cp in copies:
        cp.wait()


def solution(mesh):
    n_gx, n_gy = mesh.shape["gx"], mesh.shape["gy"]
    kernel = make_kernel(n_gx, n_gy)

    def local(coarse_state, fine_state, patch_source, patch_live):
        coarse = jnp.transpose(coarse_state, (1, 2, 0, 3))
        source = jnp.transpose(patch_source, (0, 2, 1))
        live = jnp.transpose(patch_live, (0, 2, 1))
        coarse, fine, source, live = (
            pltpu.with_memory_space_constraint(v, pltpu.HBM) for v in (coarse, fine_state, source, live)
        )
        v = pltpu.VMEM
        hbm = pl.BlockSpec(memory_space=pltpu.HBM)
        vmem = pl.BlockSpec(memory_space=pltpu.VMEM)
        coarse_out, fine_out = pl.pallas_call(
            kernel,
            out_shape=(
                pltpu.VMEM(coarse.shape, F32),
                pltpu.VMEM(fine_state.shape, F32),
            ),
            in_specs=[hbm] * 4,
            out_specs=(vmem, vmem),
            scratch_shapes=[
                v((SIDE, 10, 3, 8, L), F32),
                v((10, 8, 3, 8, L), F32),
                v((F, 4 * CAP * L), F32),
                v((SIDE, 8, 3, 8, L), F32),
                v((SIDE, 8, 8, L), F32),
                v((3, SIDE, F, 8, L), F32),
                v((3, SIDE, F, 8, L), F32),
                v((SIDE, F, 8, L), F32),
                v((SIDE, F, 8, L), F32),
                v((SIDE, F, 8, L), F32),
                v((SIDE, F, 8, L), F32),
                v((SIDE, SIDE, 8, L), F32),
                v((CAP, 8, L), F32),
                v((CAP, 8, L), F32),
                v((2 * CAP, 4, 8, L), F32),
                v((2 * CAP, 4, 8, L), F32),
                v((CAP, 4, 8, L), F32),
                v((3, 2 * CAP * 32, L), F32),
                v((n_gy, 5, 8, L), F32),
                v((n_gy, 5, 8, L), F32),
                v((n_gy, 8, L), F32),
                v((n_gy, 8, L), F32),
                v((L, L), BF16),
                v((L, 3 * L), BF16),
                v((3 * L, L), BF16),
                v((L, L), BF16),
                v((L, L), BF16),
                v((L, L), BF16),
                v((4, CAP * 32, L), F32),
                v((2, CAP * 32, L), F32),
                pltpu.SMEM((CAP, n_gy), jnp.int32),
                pltpu.SMEM((CAP, n_gy), jnp.int32),
                pltpu.SMEM((n_gy,), jnp.int32),
                pltpu.SMEM((n_gy,), jnp.int32),
                pltpu.SemaphoreType.DMA((2, 3)),
                pltpu.SemaphoreType.DMA,
                pltpu.SemaphoreType.DMA((2,)),
                pltpu.SemaphoreType.DMA((3, 4)),
                pltpu.SemaphoreType.DMA((3, 4)),
                pltpu.SemaphoreType.DMA((2,)),
                pltpu.SemaphoreType.DMA((2,)),
            ],
            compiler_params=pltpu.CompilerParams(
                collective_id=0, has_side_effects=True, vmem_limit_bytes=48 * 2**20
            ),
        )(coarse, fine, source, live)
        coarse_out, fine_out = (
            pltpu.with_memory_space_constraint(v, pltpu.VMEM) for v in (coarse_out, fine_out)
        )
        coarse_out, fine_out = pl.pallas_call(
            hand_over,
            out_shape=(
                jax.ShapeDtypeStruct(coarse.shape, F32),
                jax.ShapeDtypeStruct(fine_state.shape, F32),
            ),
            in_specs=[vmem] * 2,
            out_specs=(hbm, hbm),
            scratch_shapes=[pltpu.SemaphoreType.DMA((2,))],
        )(coarse_out, fine_out)
        return jnp.transpose(coarse_out, (2, 0, 1, 3)), fine_out

    return jax.shard_map(
        local,
        mesh=mesh,
        in_specs=(P(None, "gx", "gy", None), P(None, ("gx", "gy")), P(), P()),
        out_specs=(P(None, "gx", "gy", None), P(None, ("gx", "gy"))),
        check_vma=False,
    )
```

time: 30.8 us -> 24.5 us (0.80)
  local copies, waits for them, and re-layouts: 4.75 us -> 0 us
  Pallas kernels: 25.1 us -> 23.8 us
    unnamed x10 -> x0, local copies, waits for them, and re-layouts: 4.75 us -> none
    pallas_call x1 -> x2, Pallas kernels: 25.1 us -> 23.8 us  [the longest x1 23 us: local(): pl.pallas_call(kernel, out_shape=(pltpu.VMEM(coarse.shape, F32), pltpu.VM...]
where the time goes in v2:
time: 24.5 us; the launch traced here: 24.4 us
  Pallas kernels  23.8 us (97%)
  between operations  0.64 us (3%)
    pallas_call x1, Pallas kernels, local(): pl.pallas_call(kernel, out_shape=(pltpu.VMEM(coarse.shape, F32), pltpu.VM...  23 us
    pallas_call x1, Pallas kernels, local(): pl.pallas_call(hand_over, out_shape=(jax.ShapeDtypeStruct(coarse.shape, F...  0.79 us

profile of v2, /device:TPU:1, one launch (start us, length us, event | category | flops | bytes accessed | tf_op | source)
XLA Modules:
  0.0 24.4 jit_solution(2331122811923554593)
XLA Ops:
  0.6 23.0 %shard_map.59 = (f32[6,6,7,384]{3,2,1,0:T(8,128)S(1)}, f32[7,2048]{1,0:T(8,128)S(1)}) custom-call(f32[6,6,7,384]{3,2,1,0:T(8,128)} %bitcast.4, f32[7,2048]{1,0:T(8,128)} %fine.1, s32[16,4,16]{2,1,0:T(4,128)} %bitcast.5, s32[16,4,16]{2,1,0:T(4,128)} %bitcast.6), custom_call_target="tpu_custom_call" | custom-call | tf_op jit(solution)/shard_map/pallas_call | solution.py:587
  23.6 0.8 %shard_map.60 = (f32[6,6,7,384]{3,2,1,0:T(8,128)}, f32[7,2048]{1,0:T(8,128)}) custom-call(f32[6,6,7,384]{3,2,1,0:T(8,128)S(1)} %get-tuple-element.6.coarse, f32[7,2048]{1,0:T(8,128)S(1)} %get-tuple-element.7.fine), custom_call_target="tpu_custom_call" | custom-call | tf_op jit(solution)/shard_map/pallas_call | solution.py:645

commit v3 on v2

--- a/solution.py
+++ b/solution.py
@@ -34,6 +34,10 @@
     out = jnp.dot(hi, e, preferred_element_type=F32)
     out = out + jnp.dot(mid, e, preferred_element_type=F32)
     return out + jnp.dot(low, e, preferred_element_type=F32)
+
+
+def pick(tile, index):
+    return jnp.take_along_axis(tile, index, axis=1, mode="promise_in_bounds")
 
 
 def minmod(a, b):
@@ -77,8 +81,8 @@
 def make_kernel(n_gx, n_gy):
     def kernel(
         coarse, fine, source, live, coarse_out, fine_out,
-        S, OWN, FIN, BASE, NEWC, PZ, MZ, PX, MX, CH, CM, BB, MO, MN, GL, FS, FT, GG, SB1, RB1, SB2, RB2,
-        EZ, EG, WD, WX, E2, E2X, LW, TT, src_s, live_s, kf_s, kg_s,
+        S, OWN, FIN, BASE, NEWC, PZ, MZ, PX, MX, CH, CM, CX, MO, MN, FS, FT, GG, SB0, RB0, SB1, RB1, SB2, RB2,
+        WD, WX, LW, TT, src_s, live_s, kf_s, kg_s,
         in_sem, fin_sem, tab_sem, h_send, h_recv, m_send, m_recv,
     ):
         a = lax.axis_index("gx")
@@ -116,21 +120,6 @@
         ]
         for cp in tabs + own[:1] + [fin_cp] + own[1:]:
             cp.start()
-
-        row = iota((L, L), 0)
-        col = iota((L, L), 1)
-        c32 = col & 31
-        s32 = col >> 5
-        zc = jnp.where(
-            c32 < 4, 0, jnp.where(c32 < 8, 5, jnp.where(c32 < 12, c32 - 7, jnp.where(c32 < 16, c32 - 11, (c32 & 3) + 1)))
-        )
-        EZ[...] = (row == 6 * s32 + zc).astype(F32).astype(BF16)
-        fy = (col >> 3) & 7
-        fz = col & 7
-        cz, cy = fz >> 1, fy >> 1
-        EG[:, 0:L] = (row == jnp.where(fz < 4, 0, 4) + cy).astype(F32).astype(BF16)
-        EG[:, L : 2 * L] = (row == jnp.where(fy < 4, 8, 12) + cz).astype(F32).astype(BF16)
-        EG[:, 2 * L : 3 * L] = (row == 16 + cy * 4 + cz).astype(F32).astype(BF16)
 
         for cp in tabs:
             cp.wait()
@@ -165,19 +154,22 @@
         )
         low16 = lc < 16
 
-        def ghost_messages(tiles, dst):
-            BB[...] = exact_dot(tiles.reshape(SIDE * SIDE * 8, L), EZ[...]).reshape(SIDE, SIDE, 8, L)
-            merged = []
-            for X in range(4):
-                acc = BB[X + 1, 0]
-                for y in range(1, 6):
-                    acc = jnp.where(low16 & (ly == y), BB[X + 1, y], acc)
-                if X in (0, 3):
-                    for y in range(1, 5):
-                        acc = jnp.where(
-                            jnp.logical_not(low16) & (ly == y), BB[0 if X == 0 else 5, y], acc
-                        )
-                merged.append(acc)
+        lzc = jnp.where(
+            lc < 4, 0, jnp.where(lc < 8, 5, jnp.where(lc < 12, lc - 7, jnp.where(lc < 16, lc - 11, (lc & 3) + 1)))
+        )
+        to_code = 6 * ls + lzc
+
+        def merge(tile, X):
+            acc = pick(tile(X + 1, 0), to_code)
+            for y in range(1, 6):
+                acc = jnp.where(low16 & (ly == y), pick(tile(X + 1, y), to_code), acc)
+            if X in (0, 3):
+                for y in range(1, 5):
+                    part = pick(tile(0 if X == 0 else 5, y), to_code)
+                    acc = jnp.where(jnp.logical_not(low16) & (ly == y), part, acc)
+            return acc
+
+        def ghost_messages(merged, dst):
             for k in range(CAP):
                 acc = None
                 for X in range(4):
@@ -187,19 +179,17 @@
                 dst[k] = acc
 
         own[0].wait()
-        ghost_messages(OWN[2:8, 0:SIDE, 0], MO)
+        ghost_messages([merge(lambda x, y: OWN[x + 2, y, 0], X) for X in range(4)], MO)
         fin_cp.wait()
         for t in range(4 * CAP):
             FT[t // 4, t % 4, 0:F, :] = FIN[:, t * L : (t + 1) * L]
 
-        def fill1(o, buf):
-            buf[o, 0:4] = FT[kf_s[o]]
-            buf[o, 4] = MO[kg_s[o]]
-
-        fill1(0, RB1)
+        RB0[0] = MO[kg_s[0]]
+        RB1[0] = FT[kf_s[0]]
 
         def fill(o, _):
-            fill1(o, SB1)
+            SB0[o] = MO[kg_s[o]]
+            SB1[o] = FT[kf_s[o]]
             return 0
 
         lax.fori_loop(1, n_gy, fill, 0)
@@ -207,21 +197,23 @@
             cp.wait()
         pl.semaphore_wait(barrier, n_gy + 1)
 
-        def halo(j):
+        def halo(lo, hi, sides=(0, 1, 2, 3)):
             copies = []
             for h, (buf, src, dst, dev) in enumerate(
                 (
-                    (OWN, OWN.at[6:8, 0:SIDE, j, 0:F, :], OWN.at[0:2, 0:SIDE, j, 0:F, :], (up_a, b)),
-                    (OWN, OWN.at[2:4, 0:SIDE, j, 0:F, :], OWN.at[8:10, 0:SIDE, j, 0:F, :], (dn_a, b)),
-                    (S, S.at[:, 6:8, j, 0:F, :], S.at[:, 0:2, j, 0:F, :], (a, up_b)),
-                    (S, S.at[:, 2:4, j, 0:F, :], S.at[:, 8:10, j, 0:F, :], (a, dn_b)),
+                    (OWN, OWN.at[6:8, 0:SIDE, lo:hi, 0:F, :], OWN.at[0:2, 0:SIDE, lo:hi, 0:F, :], (up_a, b)),
+                    (OWN, OWN.at[2:4, 0:SIDE, lo:hi, 0:F, :], OWN.at[8:10, 0:SIDE, lo:hi, 0:F, :], (dn_a, b)),
+                    (S, S.at[:, 6:8, lo:hi, 0:F, :], S.at[:, 0:2, lo:hi, 0:F, :], (a, up_b)),
+                    (S, S.at[:, 2:4, lo:hi, 0:F, :], S.at[:, 8:10, lo:hi, 0:F, :], (a, dn_b)),
                 )
             ):
+                if h not in sides:
+                    continue
                 cp = pltpu.make_async_remote_copy(
                     src_ref=src,
                     dst_ref=dst,
-                    send_sem=h_send.at[j, h],
-                    recv_sem=h_recv.at[j, h],
+                    send_sem=h_send.at[lo, h],
+                    recv_sem=h_recv.at[lo, h],
                     device_id=dev,
                     device_id_type=MESH,
                 )
@@ -229,22 +221,26 @@
                 copies.append(cp)
             return copies
 
-        halos = halo(0)
-
-        def send1(i, _):
-            o = partner(i)
-            pltpu.make_async_remote_copy(
-                src_ref=SB1.at[o, :, 0:F, :],
-                dst_ref=RB1.at[o, :, 0:F, :],
-                send_sem=m_send.at[0],
-                recv_sem=m_recv.at[0],
-                device_id=(a, lax.rem(b + o, n_gy)),
-                device_id_type=MESH,
-            ).start()
-            return 0
-
-        lax.fori_loop(0, n_gy - 1, send1, 0)
-        halos += halo(1) + halo(2)
+        halos = halo(0, 1)
+
+        def send_to_partners(src, dst, sem):
+            def send(i, _):
+                o = partner(i)
+                pltpu.make_async_remote_copy(
+                    src_ref=src(o),
+                    dst_ref=dst(o),
+                    send_sem=m_send.at[sem],
+                    recv_sem=m_recv.at[sem],
+                    device_id=(a, lax.rem(b + o, n_gy)),
+                    device_id_type=MESH,
+                ).start()
+                return 0
+
+            lax.fori_loop(0, n_gy - 1, send, 0)
+
+        send_to_partners(lambda o: SB0.at[o, 0:F, :], lambda o: RB0.at[o, 0:F, :], 0)
+        send_to_partners(lambda o: SB1.at[o, :, 0:F, :], lambda o: RB1.at[o, :, 0:F, :], 1)
+        halos_x = halo(1, 3, (0, 1))
 
         def cells(x, j):
             start = ((x + 2) * 24 + j) * 8
@@ -276,6 +272,9 @@
                 PX[x, f] = plus[f]
                 MX[x, f] = minus[f]
 
+        row = iota((L, L), 0)
+        col = iota((L, L), 1)
+        c32 = col & 31
         ry = (row >> 3) & 7
         rz = row & 7
         rzc, ryc = rz >> 1, ry >> 1
@@ -293,13 +292,6 @@
         for i, w in enumerate((wa, wz, wy)):
             WD[i * L : (i + 1) * L, :] = jnp.where(w, 0.125, 0.0).astype(BF16)
         WX[...] = jnp.where((ryc == (c32 >> 2)) & (rzc == (c32 & 3)), 0.125, 0.0).astype(BF16)
-        r32 = row & 31
-        rs = row >> 5
-        r6 = (r32 * 43) >> 8
-        rzv = jnp.where(r32 < 24, r32 - 6 * r6, (r32 & 3) + 1)
-        E2[...] = (col == 6 * rs + rzv).astype(F32).astype(BF16)
-        E2X[...] = (col == 6 * rs + (r32 & 3) + 1).astype(F32).astype(BF16)
-
         slot24 = (lane >= 6).astype(jnp.int32) + (lane >= 12).astype(jnp.int32) + (lane >= 18).astype(jnp.int32)
         zpos = lane - 6 * slot24
         alive_lane = jnp.where(
@@ -342,19 +334,13 @@
                         jnp.where(z_low, 0.0, z_up) - jnp.where(z_high, 0.0, z_lo)
                     )
                 CM[x, f] = whole
-        halos[0].wait_recv()
-        halos[1].wait_recv()
-        ends = {x: x_split(x, 0) for x in (-1, 0, 5, 6)}
-
-        def plus_of(x, f):
-            return ends[x][0][f] if x in ends else PX[x, f]
-
-        def minus_of(x, f):
-            return ends[x][1][f] if x in ends else MX[x, f]
-
-        lower = [plus_of(-1, f) + minus_of(0, f) for f in range(F)]
-        for x in range(SIDE):
-            upper = [plus_of(x, f) + minus_of(x + 1, f) for f in range(F)]
+        def face(plus, minus):
+            return [p + m for p, m in zip(plus, minus)]
+
+        def stored(buf, x):
+            return [buf[x, f] for f in range(F)]
+
+        def finish(x, lower, upper):
             new = react(cells(x, 0), [CH[x, f] + (upper[f] - lower[f]) for f in range(F)], 0.05)
             for f in range(F):
                 put(NEWC, x * 64 + f, 8, 8, new[f])
@@ -364,68 +350,76 @@
                 elif x == 5:
                     lo_m = jnp.where(inner, 0.0, lo_m)
                 CM[x, f] = CM[x, f] + (up_m - lo_m)
-            lower = upper
-
-        ghost_messages(NEWC[:, 0:SIDE], MN)
+
+        face12 = face(stored(PX, 1), stored(MX, 2))
+        face23 = face(stored(PX, 2), stored(MX, 3))
+        face34 = face(stored(PX, 3), stored(MX, 4))
+        finish(2, face12, face23)
+        finish(3, face23, face34)
+
+        def new_tile(x, y):
+            return NEWC[x, y]
+
+        mid = [merge(new_tile, 1), merge(new_tile, 2)]
+        halos[0].wait_recv()
+        plus_m1, _ = x_split(-1, 0)
+        plus_0, minus_0 = x_split(0, 0)
+        face01 = face(plus_0, stored(MX, 1))
+        finish(0, face(plus_m1, minus_0), face01)
+        finish(1, face01, face(stored(PX, 1), stored(MX, 2)))
+        first = merge(new_tile, 0)
+        halos[1].wait_recv()
+        plus_5, minus_5 = x_split(5, 0)
+        _, minus_6 = x_split(6, 0)
+        face45 = face(stored(PX, 4), minus_5)
+        finish(4, face(stored(PX, 3), stored(MX, 4)), face45)
+        finish(5, face45, face(plus_5, minus_6))
+        ghost_messages([first] + mid + [merge(new_tile, 3)], MN)
         RB2[0] = MN[kg_s[0]]
-
-        def send2(i, _):
-            o = partner(i)
+        for o in range(1, n_gy):
             SB2[o] = MN[kg_s[o]]
-            pltpu.make_async_remote_copy(
-                src_ref=SB2.at[o, 0:F, :],
-                dst_ref=RB2.at[o, 0:F, :],
-                send_sem=m_send.at[1],
-                recv_sem=m_recv.at[1],
-                device_id=(a, lax.rem(b + o, n_gy)),
-                device_id_type=MESH,
-            ).start()
-            return 0
-
-        lax.fori_loop(0, n_gy - 1, send2, 0)
+        send_to_partners(lambda o: SB2.at[o, 0:F, :], lambda o: RB2.at[o, 0:F, :], 2)
 
         for x in range(SIDE):
             store(x, zero, react(cells(x, 0), [CM[x, f] for f in range(F)], 0.05))
-        for cp in halos[4:]:
+        halos_y = halo(1, 3, (2, 3))
+        for cp in halos_x:
             cp.wait_recv()
 
-        def rest(j, _):
+        def rest_xz(j, _):
             before = x_split(-1, j)[0]
             lower = None
             for x in range(SIDE + 1):
                 plus, minus = x_split(x, j)
-                upper = [p + m for p, m in zip(before, minus)]
+                upper = face(before, minus)
                 if lower is not None:
-                    y_lo, y_up = y_parts(x - 1, j)
-                    change = []
                     for f in range(F):
                         z_lo, z_up = z_faces(x - 1, f, j)
-                        change.append((upper[f] - lower[f]) + (y_up[f] - y_lo[f]) + (z_up - z_lo))
-                    store(x - 1, j, react(cells(x - 1, j), change, 0.05))
+                        CX[j, x - 1, f] = (upper[f] - lower[f]) + (z_up - z_lo)
                 before, lower = plus, upper
             return 0
 
-        lax.fori_loop(1, 3, rest, 0)
-        for x in range(SIDE):
-            for y in range(SIDE):
-                for j in (1, 2):
-                    coarse_out[x, y, :, j * L : (j + 1) * L] = BASE[x, y, j, 0:F]
+        lax.fori_loop(1, 3, rest_xz, 0)
 
         def wait_messages(whole, sem):
             pltpu.make_async_copy(whole, whole, sem).wait()
 
         my_src = [lax.rem(b + n_gy - src_s[k, b], n_gy) for k in range(CAP)]
         my_live = [live_s[k, b] for k in range(CAP)]
+
+        tz, ty = lane & 7, (lane >> 3) & 7
+        to_cell = (
+            jnp.where(tz < 4, 0, 4) + (ty >> 1),
+            jnp.where(ty < 4, 8, 12) + (tz >> 1),
+            16 + (ty >> 1) * 4 + (tz >> 1),
+        )
 
         def ghost_fields(messages):
             n = len(messages)
             for k in range(n):
                 for X in range(4):
-                    tile = messages[k]
-                    GL[k, X] = tile if X == 0 else pltpu.roll(tile, L - 32 * X, 1)
-            expanded = exact_dot(GL[0:n].reshape(n * 32, L), EG[...])
-            for i in range(3):
-                GG[i, 0 : n * 32] = expanded[:, i * L : (i + 1) * L]
+                    for i in range(3):
+                        GG[i, (k * 4 + X) * 8 : (k * 4 + X) * 8 + 8] = pick(messages[k], to_cell[i] + 32 * X)
             return [[GG[i, pl.ds(f, 4 * n, stride=8), :] for f in range(F)] for i in range(3)]
 
         def lane_down(step):
@@ -477,26 +471,26 @@
                 )
             return react(u, change, 0.025), faces
 
-        wait_messages(RB1.at[1:n_gy, :, 0:F, :], m_recv.at[0])
+        wait_messages(RB0.at[1:n_gy, 0:F, :], m_recv.at[0])
         for k in range(CAP):
-            FS[k] = RB1[owner[k], 0:4]
             FS[CAP + k] = FT[k]
-        old = [MO[k] for k in range(CAP)] + [RB1[my_src[k], 4] for k in range(CAP)]
-        u0 = [take(FS, f, 8 * CAP, 8) for f in range(F)]
-        u1, faces1 = substep(u0, ghost_fields(old))
+        u0 = [take(FS, CAP * 32 + f, 16, 8) for f in range(F)]
+        u1, _ = substep(u0, ghost_fields([RB0[my_src[k]] for k in range(CAP)]))
         for f in range(F):
-            put(FS, f, 8 * CAP, 8, u1[f])
-            for i in range(3):
-                LW[1 + i, pl.ds(f, 16, stride=8), :] = faces1[i][f]
-
-        mean = [0.5 * (MO[k] + MN[k]) for k in range(CAP)]
-        u1 = [take(FS, f, 16, 8) for f in range(F)]
-        u2, faces2 = substep(u1, ghost_fields(mean))
+            put(FS, CAP * 32 + f, 16, 8, u1[f])
+
+        tile_old = ghost_fields([MO[k] for k in range(CAP)])
+        wait_messages(RB1.at[1:n_gy, :, 0:F, :], m_recv.at[1])
+        for k in range(CAP):
+            FS[k] = RB1[owner[k]]
+        u0 = [take(FS, f, 16, 8) for f in range(F)]
+        u1, faces1 = substep(u0, tile_old)
+        u2, faces2 = substep(u1, ghost_fields([0.5 * (MO[k] + MN[k]) for k in range(CAP)]))
         for f in range(F):
             rows = pl.ds(f, 16, stride=8)
             LW[0, rows, :] = u2[f]
             for i in range(3):
-                LW[1 + i, rows, :] = LW[1 + i, rows, :] + faces2[i][f]
+                LW[1 + i, rows, :] = faces1[i][f] + faces2[i][f]
 
         TT[0] = exact_dot(jnp.concatenate([LW[0], LW[1], LW[2]], axis=1), WD[...])
         TT[1] = exact_dot(LW[3], WX[...])
@@ -509,38 +503,43 @@
                 acc = jnp.where(ls == k, TT[i, pl.ds((k * 4 + X) * 8, 8), :], acc)
             return jnp.where(keep, acc, 0.0)
 
-        l6 = (lc * 43) >> 8
-        lyv = jnp.where(lc < 24, l6 + 1, jnp.where(lc < 28, 0, 5))
-        blocks = []
-        for X in range(4):
-            t = by_slot(0, X)
-            for y in range(6):
-                blocks.append(jnp.where(lyv == y, t, 0.0))
-        inside = exact_dot(jnp.concatenate(blocks, axis=0), E2[...])
-        lxy = (lc >> 2) + 1
-        blocks = []
-        for X in (0, 3):
-            t = by_slot(1, X)
-            for y in range(1, 5):
-                blocks.append(jnp.where(lxy == y, t, 0.0))
-        across = exact_dot(jnp.concatenate(blocks, axis=0), E2X[...])
+        z_mid = (lane < 24) & (zpos >= 1) & (zpos <= 4)
+        base_code = jnp.where(lane < 24, 32 * slot24, 0)
+        tt = [by_slot(0, X) for X in range(4)]
+        tx = {0: by_slot(1, 0), 5: by_slot(1, 3)}
         for x in range(SIDE):
             for y in range(SIDE):
                 tile = BASE[x, y, 0]
                 if 1 <= x <= 4:
-                    i = ((x - 1) * 6 + y) * 8
-                    part = inside[i : i + 8]
                     if 1 <= y <= 4:
-                        tile = jnp.where(zin, part, tile + part)
+                        part = pick(tt[x - 1], base_code + jnp.where(lane < 24, (y - 1) * 6 + zpos, 0))
+                        tile = jnp.where(zin, part, jnp.where(lane < 24, tile + part, tile))
                     else:
-                        tile = tile + part
+                        code = (24 if y == 0 else 28) + jnp.where(z_mid, zpos - 1, 0)
+                        tile = jnp.where(z_mid, tile + pick(tt[x - 1], base_code + code), tile)
                 elif 1 <= y <= 4:
-                    i = ((0 if x == 0 else 4) + y - 1) * 8
-                    tile = tile + across[i : i + 8]
+                    code = (y - 1) * 4 + jnp.where(z_mid, zpos - 1, 0)
+                    tile = jnp.where(z_mid, tile + pick(tx[x], base_code + code), tile)
                 coarse_out[x, y, :, 0:L] = tile[0:F]
 
-        wait_messages(RB2.at[1:n_gy, 0:F, :], m_recv.at[1])
-        mean = [0.5 * (RB1[my_src[k], 4] + RB2[my_src[k]]) for k in range(CAP)]
+        for cp in halos_y:
+            cp.wait_recv()
+
+        def rest_y(j, _):
+            for x in range(SIDE):
+                y_lo, y_up = y_parts(x, j)
+                change = [CX[j, x, f] + (y_up[f] - y_lo[f]) for f in range(F)]
+                store(x, j, react(cells(x, j), change, 0.05))
+            return 0
+
+        lax.fori_loop(1, 3, rest_y, 0)
+        for x in range(SIDE):
+            for y in range(SIDE):
+                for j in (1, 2):
+                    coarse_out[x, y, :, j * L : (j + 1) * L] = BASE[x, y, j, 0:F]
+
+        wait_messages(RB2.at[1:n_gy, 0:F, :], m_recv.at[2])
+        mean = [0.5 * (RB0[my_src[k]] + RB2[my_src[k]]) for k in range(CAP)]
         u1 = [take(FS, CAP * 32 + f, 16, 8) for f in range(F)]
         u2, _ = substep(u1, ghost_fields(mean))
         for f in range(F):
@@ -551,10 +550,11 @@
                 my_live[k] == 1, FS[CAP + k, t % 4, 0:F, :], FT[k, t % 4, 0:F, :]
             )
 
-        for cp in halos:
+        for cp in halos + halos_x + halos_y:
             cp.wait_send()
-        wait_messages(SB1.at[1:n_gy, :, 0:F, :], m_send.at[0])
-        wait_messages(SB2.at[1:n_gy, 0:F, :], m_send.at[1])
+        wait_messages(SB0.at[1:n_gy, 0:F, :], m_send.at[0])
+        wait_messages(SB1.at[1:n_gy, :, 0:F, :], m_send.at[1])
+        wait_messages(SB2.at[1:n_gy, 0:F, :], m_send.at[2])
 
     return kernel
 
@@ -604,22 +604,19 @@
                 v((SIDE, F, 8, L), F32),
                 v((SIDE, F, 8, L), F32),
                 v((SIDE, F, 8, L), F32),
-                v((SIDE, SIDE, 8, L), F32),
+                v((3, SIDE, F, 8, L), F32),
                 v((CAP, 8, L), F32),
                 v((CAP, 8, L), F32),
                 v((2 * CAP, 4, 8, L), F32),
-                v((2 * CAP, 4, 8, L), F32),
                 v((CAP, 4, 8, L), F32),
                 v((3, 2 * CAP * 32, L), F32),
-                v((n_gy, 5, 8, L), F32),
-                v((n_gy, 5, 8, L), F32),
                 v((n_gy, 8, L), F32),
                 v((n_gy, 8, L), F32),
-                v((L, L), BF16),
-                v((L, 3 * L), BF16),
+                v((n_gy, 4, 8, L), F32),
+                v((n_gy, 4, 8, L), F32),
+                v((n_gy, 8, L), F32),
+                v((n_gy, 8, L), F32),
                 v((3 * L, L), BF16),
-                v((L, L), BF16),
-                v((L, L), BF16),
                 v((L, L), BF16),
                 v((4, CAP * 32, L), F32),
                 v((2, CAP * 32, L), F32),
@@ -630,10 +627,10 @@
                 pltpu.SemaphoreType.DMA((2, 3)),
                 pltpu.SemaphoreType.DMA,
                 pltpu.SemaphoreType.DMA((2,)),
-                pltpu.SemaphoreType.DMA((3, 4)),
-                pltpu.SemaphoreType.DMA((3, 4)),
-                pltpu.SemaphoreType.DMA((2,)),
-                pltpu.SemaphoreType.DMA((2,)),
+                pltpu.SemaphoreType.DMA((2, 4)),
+                pltpu.SemaphoreType.DMA((2, 4)),
+                pltpu.SemaphoreType.DMA((3,)),
+                pltpu.SemaphoreType.DMA((3,)),
             ],
             compiler_params=pltpu.CompilerParams(
                 collective_id=0, has_side_effects=True, vmem_limit_bytes=48 * 2**20

time: 24.5 us -> 23.7 us (0.967)
  Pallas kernels: 23.8 us -> 23 us
    pallas_call x1, Pallas kernels: 23 us -> 22.2 us  [local(): pl.pallas_call(kernel, out_shape=(pltpu.VMEM(coarse.shape, F32), pltpu.VM...]
where the time goes in v3:
time: 23.7 us
  Pallas kernels  23 us (97%)
  between operations  0.64 us (3%)
    pallas_call x1, Pallas kernels, local(): pl.pallas_call(kernel, out_shape=(pltpu.VMEM(coarse.shape, F32), pltpu.VM...  22.2 us
    pallas_call x1, Pallas kernels, local(): pl.pallas_call(hand_over, out_shape=(jax.ShapeDtypeStruct(coarse.shape, F...  0.79 us

profile of v3, /device:TPU:1, one launch (start us, length us, event | category | flops | bytes accessed | tf_op | source)
XLA Modules:
  0.0 23.7 jit_solution(9456107475961531695)
XLA Ops:
  0.6 22.2 %shard_map.59 = (f32[6,6,7,384]{3,2,1,0:T(8,128)S(1)}, f32[7,2048]{1,0:T(8,128)S(1)}) custom-call(f32[6,6,7,384]{3,2,1,0:T(8,128)} %bitcast.4, f32[7,2048]{1,0:T(8,128)} %fine.1, s32[16,4,16]{2,1,0:T(4,128)} %bitcast.5, s32[16,4,16]{2,1,0:T(4,128)} %bitcast.6), custom_call_target="tpu_custom_call" | custom-call | tf_op jit(solution)/shard_map/pallas_call | solution.py:587
  22.9 0.8 %shard_map.60 = (f32[6,6,7,384]{3,2,1,0:T(8,128)}, f32[7,2048]{1,0:T(8,128)}) custom-call(f32[6,6,7,384]{3,2,1,0:T(8,128)S(1)} %get-tuple-element.6.coarse, f32[7,2048]{1,0:T(8,128)S(1)} %get-tuple-element.7.fine), custom_call_target="tpu_custom_call" | custom-call | tf_op jit(solution)/shard_map/pallas_call | solution.py:642

commit v4 on v3

--- a/solution.py
+++ b/solution.py
@@ -81,7 +81,7 @@
 def make_kernel(n_gx, n_gy):
     def kernel(
         coarse, fine, source, live, coarse_out, fine_out,
-        S, OWN, FIN, BASE, NEWC, PZ, MZ, PX, MX, CH, CM, CX, MO, MN, FS, FT, GG, SB0, RB0, SB1, RB1, SB2, RB2,
+        S, OWN, FIN, BASE, NEWC, PZ, MZ, PX, MX, CH, CM, CX, MO, MN, MOP, MNP, FS, FT, GG, SB0, RB0, SB1, RB1, SB2, RB2,
         WD, WX, LW, TT, src_s, live_s, kf_s, kg_s,
         in_sem, fin_sem, tab_sem, h_send, h_recv, m_send, m_recv,
     ):
@@ -169,7 +169,25 @@
                     acc = jnp.where(jnp.logical_not(low16) & (ly == y), part, acc)
             return acc
 
-        def ghost_messages(merged, dst):
+        hole = (lane >= 48) & (lane < 64)
+        from_lane = jnp.where(sub < 3, 16 * sub, jnp.where(sub == 3, 64, 16 * sub + 32))
+        to_hole = jnp.where(hole & (sub < 6), from_lane + lane - 48, lane)
+        from_hole = 48 + (lane & 15)
+        part16 = lane >> 4
+        from_row = jnp.where(
+            part16 < 3, part16, jnp.where(part16 == 4, 3, jnp.where(part16 >= 6, part16 - 2, 8))
+        )
+
+        def pack(tile):
+            return jnp.where(hole, pick(jnp.broadcast_to(tile[6:7], (8, L)), to_hole), tile)
+
+        def unpack(tile):
+            last = jnp.where(sub == from_row, pick(tile, from_hole), 0.0)
+            for step in (4, 2, 1):
+                last = last + pltpu.roll(last, step, 0)
+            return jnp.where(sub == 6, last, tile)
+
+        def ghost_messages(merged, dst, packed):
             for k in range(CAP):
                 acc = None
                 for X in range(4):
@@ -177,18 +195,19 @@
                     part = merged[X] if shift == 0 else pltpu.roll(merged[X], shift, 1)
                     acc = part if acc is None else jnp.where(ls == X, part, acc)
                 dst[k] = acc
+                packed[k] = pack(acc)
 
         own[0].wait()
-        ghost_messages([merge(lambda x, y: OWN[x + 2, y, 0], X) for X in range(4)], MO)
+        ghost_messages([merge(lambda x, y: OWN[x + 2, y, 0], X) for X in range(4)], MO, MOP)
         fin_cp.wait()
         for t in range(4 * CAP):
             FT[t // 4, t % 4, 0:F, :] = FIN[:, t * L : (t + 1) * L]
 
-        RB0[0] = MO[kg_s[0]]
+        RB0[0] = MOP[kg_s[0]]
         RB1[0] = FT[kf_s[0]]
 
         def fill(o, _):
-            SB0[o] = MO[kg_s[o]]
+            SB0[o] = MOP[kg_s[o]]
             SB1[o] = FT[kf_s[o]]
             return 0
 
@@ -238,7 +257,7 @@
 
             lax.fori_loop(0, n_gy - 1, send, 0)
 
-        send_to_partners(lambda o: SB0.at[o, 0:F, :], lambda o: RB0.at[o, 0:F, :], 0)
+        send_to_partners(lambda o: SB0.at[o, 0 : F - 1, :], lambda o: RB0.at[o, 0 : F - 1, :], 0)
         send_to_partners(lambda o: SB1.at[o, :, 0:F, :], lambda o: RB1.at[o, :, 0:F, :], 1)
         halos_x = halo(1, 3, (0, 1))
 
@@ -374,11 +393,11 @@
         face45 = face(stored(PX, 4), minus_5)
         finish(4, face(stored(PX, 3), stored(MX, 4)), face45)
         finish(5, face45, face(plus_5, minus_6))
-        ghost_messages([first] + mid + [merge(new_tile, 3)], MN)
-        RB2[0] = MN[kg_s[0]]
+        ghost_messages([first] + mid + [merge(new_tile, 3)], MN, MNP)
+        RB2[0] = MNP[kg_s[0]]
         for o in range(1, n_gy):
-            SB2[o] = MN[kg_s[o]]
-        send_to_partners(lambda o: SB2.at[o, 0:F, :], lambda o: RB2.at[o, 0:F, :], 2)
+            SB2[o] = MNP[kg_s[o]]
+        send_to_partners(lambda o: SB2.at[o, 0 : F - 1, :], lambda o: RB2.at[o, 0 : F - 1, :], 2)
 
         for x in range(SIDE):
             store(x, zero, react(cells(x, 0), [CM[x, f] for f in range(F)], 0.05))
@@ -471,11 +490,11 @@
                 )
             return react(u, change, 0.025), faces
 
-        wait_messages(RB0.at[1:n_gy, 0:F, :], m_recv.at[0])
+        wait_messages(RB0.at[1:n_gy, 0 : F - 1, :], m_recv.at[0])
         for k in range(CAP):
             FS[CAP + k] = FT[k]
         u0 = [take(FS, CAP * 32 + f, 16, 8) for f in range(F)]
-        u1, _ = substep(u0, ghost_fields([RB0[my_src[k]] for k in range(CAP)]))
+        u1, _ = substep(u0, ghost_fields([unpack(RB0[my_src[k]]) for k in range(CAP)]))
         for f in range(F):
             put(FS, CAP * 32 + f, 16, 8, u1[f])
 
@@ -538,8 +557,8 @@
                 for j in (1, 2):
                     coarse_out[x, y, :, j * L : (j + 1) * L] = BASE[x, y, j, 0:F]
 
-        wait_messages(RB2.at[1:n_gy, 0:F, :], m_recv.at[2])
-        mean = [0.5 * (RB0[my_src[k]] + RB2[my_src[k]]) for k in range(CAP)]
+        wait_messages(RB2.at[1:n_gy, 0 : F - 1, :], m_recv.at[2])
+        mean = [unpack(0.5 * (RB0[my_src[k]] + RB2[my_src[k]])) for k in range(CAP)]
         u1 = [take(FS, CAP * 32 + f, 16, 8) for f in range(F)]
         u2, _ = substep(u1, ghost_fields(mean))
         for f in range(F):
@@ -552,9 +571,9 @@
 
         for cp in halos + halos_x + halos_y:
             cp.wait_send()
-        wait_messages(SB0.at[1:n_gy, 0:F, :], m_send.at[0])
+        wait_messages(SB0.at[1:n_gy, 0 : F - 1, :], m_send.at[0])
         wait_messages(SB1.at[1:n_gy, :, 0:F, :], m_send.at[1])
-        wait_messages(SB2.at[1:n_gy, 0:F, :], m_send.at[2])
+        wait_messages(SB2.at[1:n_gy, 0 : F - 1, :], m_send.at[2])
 
     return kernel
 
@@ -605,6 +624,8 @@
                 v((SIDE, F, 8, L), F32),
                 v((SIDE, F, 8, L), F32),
                 v((3, SIDE, F, 8, L), F32),
+                v((CAP, 8, L), F32),
+                v((CAP, 8, L), F32),
                 v((CAP, 8, L), F32),
                 v((CAP, 8, L), F32),
                 v((2 * CAP, 4, 8, L), F32),

time: 23.7 us -> 23.5 us (level)
  Pallas kernels: 23 us -> 22.7 us
    pallas_call x1, Pallas kernels: 22.2 us -> 21.9 us  [local(): pl.pallas_call(kernel, out_shape=(pltpu.VMEM(coarse.shape, F32), pltpu.VM...]
where the time goes in v4:
time: 23.5 us; the launch traced here: 23.4 us
  Pallas kernels  22.7 us (97%)
  between operations  0.64 us (3%)
    pallas_call x1, Pallas kernels, local(): pl.pallas_call(kernel, out_shape=(pltpu.VMEM(coarse.shape, F32), pltpu.VM...  21.9 us
    pallas_call x1, Pallas kernels, local(): pl.pallas_call(hand_over, out_shape=(jax.ShapeDtypeStruct(coarse.shape, F...  0.79 us

profile of v4, /device:TPU:1, one launch (start us, length us, event | category | flops | bytes accessed | tf_op | source)
XLA Modules:
  0.0 23.4 jit_solution(14167004905132606180)
XLA Ops:
  0.6 21.9 %shard_map.59 = (f32[6,6,7,384]{3,2,1,0:T(8,128)S(1)}, f32[7,2048]{1,0:T(8,128)S(1)}) custom-call(f32[6,6,7,384]{3,2,1,0:T(8,128)} %bitcast.4, f32[7,2048]{1,0:T(8,128)} %fine.1, s32[16,4,16]{2,1,0:T(4,128)} %bitcast.5, s32[16,4,16]{2,1,0:T(4,128)} %bitcast.6), custom_call_target="tpu_custom_call" | custom-call | tf_op jit(solution)/shard_map/pallas_call | solution.py:606
  22.6 0.8 %shard_map.60 = (f32[6,6,7,384]{3,2,1,0:T(8,128)}, f32[7,2048]{1,0:T(8,128)}) custom-call(f32[6,6,7,384]{3,2,1,0:T(8,128)S(1)} %get-tuple-element.6.coarse, f32[7,2048]{1,0:T(8,128)S(1)} %get-tuple-element.7.fine), custom_call_target="tpu_custom_call" | custom-call | tf_op jit(solution)/shard_map/pallas_call | solution.py:663

commit v5 on v4

--- a/solution.py
+++ b/solution.py
@@ -240,7 +240,7 @@
                 copies.append(cp)
             return copies
 
-        halos = halo(0, 1)
+        halos = halo(0, 1, (0, 1))
 
         def send_to_partners(src, dst, sem):
             def send(i, _):
@@ -258,6 +258,7 @@
             lax.fori_loop(0, n_gy - 1, send, 0)
 
         send_to_partners(lambda o: SB0.at[o, 0 : F - 1, :], lambda o: RB0.at[o, 0 : F - 1, :], 0)
+        halos += halo(0, 1, (2, 3))
         send_to_partners(lambda o: SB1.at[o, :, 0:F, :], lambda o: RB1.at[o, :, 0:F, :], 1)
         halos_x = halo(1, 3, (0, 1))
 

time: 23.5 us -> 23.4 us (level)
  no operation moved by 1% of the time
where the time goes in v5:
time: 23.4 us
  Pallas kernels  22.7 us (97%)
  between operations  0.64 us (3%)
    pallas_call x1, Pallas kernels, local(): pl.pallas_call(kernel, out_shape=(pltpu.VMEM(coarse.shape, F32), pltpu.VM...  21.9 us
    pallas_call x1, Pallas kernels, local(): pl.pallas_call(hand_over, out_shape=(jax.ShapeDtypeStruct(coarse.shape, F...  0.79 us

profile of v5, /device:TPU:1, one launch (start us, length us, event | category | flops | bytes accessed | tf_op | source)
XLA Modules:
  0.0 23.4 jit_solution(1007583981358205364)
XLA Ops:
  0.6 21.9 %shard_map.59 = (f32[6,6,7,384]{3,2,1,0:T(8,128)S(1)}, f32[7,2048]{1,0:T(8,128)S(1)}) custom-call(f32[6,6,7,384]{3,2,1,0:T(8,128)} %bitcast.4, f32[7,2048]{1,0:T(8,128)} %fine.1, s32[16,4,16]{2,1,0:T(4,128)} %bitcast.5, s32[16,4,16]{2,1,0:T(4,128)} %bitcast.6), custom_call_target="tpu_custom_call" | custom-call | tf_op jit(solution)/shard_map/pallas_call | solution.py:607
  22.6 0.8 %shard_map.60 = (f32[6,6,7,384]{3,2,1,0:T(8,128)}, f32[7,2048]{1,0:T(8,128)}) custom-call(f32[6,6,7,384]{3,2,1,0:T(8,128)S(1)} %get-tuple-element.6.coarse, f32[7,2048]{1,0:T(8,128)S(1)} %get-tuple-element.7.fine), custom_call_target="tpu_custom_call" | custom-call | tf_op jit(solution)/shard_map/pallas_call | solution.py:664
